TPU v7x, 32 devices: a whole 2x2x4 slice. The times are simulated.
32 devices in a mesh: parts: 2 (over y), blk: 4 (over z), grp: 2 (over x), rep: 2 (over core).
Axes of the slice: x: 2, y: 2, z: 4, core: 2. Of those that a mesh axis runs over, the one named last changes fastest.
Arguments:
- item_factors: bfloat16 [2048, 128], P(('parts', 'blk', 'grp')), parts along dimension 0, may hold values from -0.25 to 0.25
- confidence: bfloat16 [256, 4, 256], P(('parts', 'blk'), None, 'grp'), parts along dimension 0, may hold values from 0.5 to 5
- ratings: bfloat16 [256, 4, 256], P(('parts', 'blk'), None, 'grp'), parts along dimension 0, may hold values from -6 to 6
- pattern: int32 [8, 4, 2], P(('parts', 'blk'), None, 'grp'), parts along dimension 0, may hold values 0 or 1
- counts: int32 [256], P(('parts', 'blk')), parts along dimension 0, may hold values from 1 to 512
Outputs:
- user_factors: float32 [256, 128], P(('parts', 'blk', 'grp'), 'rep'), parts along dimension 0
There are 2 independent parts, one for each index of `parts`. A program takes and returns all parts, laid end to end along the dimension named above; each array names one. Nothing has to cross between parts.
All inputs are finite; a program needn't handle non-finite values. No bound on the sum of `pattern` on one device may be relied on, other than what follows from the above.
Results may differ from a plain program's by a relative error of at most 0.0031.
Values may be sent and summed in bfloat16 or wider, within the bound.
No kernel may reach another device: no remote copies, remote signals or barrier semaphores. Data moves between devices by JAX's collectives and lax.ppermute only.
A program may use at most 64 MiB of HBM per device.

v0:
```python
import jax
import jax.numpy as jnp
from jax import lax
from jax.sharding import PartitionSpec as P

CG_STEPS = 4


unobserved_weight = 0.25
regular_weight = 0.002
epsilon = 1e-06


def from_behind(block, axis, distance):
    devices = range(lax.axis_size(axis))
    route = [((i - distance) % len(devices), i) for i in devices]
    return lax.ppermute(block, axis, route)


def shards(item_factors, confidence, ratings, pattern, counts):
    tile_items, dim = item_factors.shape
    groups = lax.axis_size("grp")
    cores = lax.axis_size("rep")
    core = lax.axis_index("rep")
    half = dim // cores
    offset = core * half
    users = confidence.shape[0]
    cycle_size = lax.axis_size("blk")
    position = lax.axis_index("blk")
    flags = pattern[0, :, 0]

    def accumulate(state, piece, source):
        factor_half = lax.dynamic_slice_in_dim(piece, offset, half, 1)
        flag = lax.dynamic_index_in_dim(flags, source, 0, keepdims=False)

        def add_tile(pair_state):
            observed_now, right_now = pair_state
            weight_tile = lax.dynamic_index_in_dim(confidence, source, 1, keepdims=False).astype(
                jnp.float32
            )
            rating_tile = lax.dynamic_index_in_dim(ratings, source, 1, keepdims=False).astype(
                jnp.float32
            )
            scaled = (weight_tile[:, None, :] * factor_half.T.astype(jnp.float32)[None]).astype(
                jnp.bfloat16
            )
            observed_now = observed_now + lax.dot_general(
                scaled, piece, (((2,), (0,)), ((), ())), preferred_element_type=jnp.float32
            )
            paired = (weight_tile * rating_tile).astype(jnp.bfloat16)
            right_now = right_now + jnp.dot(paired, factor_half, preferred_element_type=jnp.float32)
            return (observed_now, right_now)

        return lax.cond(flag != 0, add_tile, lambda pair_state: pair_state, state)

    state = (jnp.zeros((users, half, dim), jnp.float32), jnp.zeros((users, half), jnp.float32))
    state = accumulate(state, item_factors, position)

    def single_turn(turn, carry):
        moving, inner = carry
        moving = from_behind(moving, "blk", 1)
        inner = accumulate(inner, moving, (position - turn) % cycle_size)
        return (moving, inner)

    unused_a, state = lax.fori_loop(1, cycle_size, single_turn, (item_factors, state))
    observed, right_side = state
    owned = users // groups
    observed, right_side = lax.psum((observed, right_side), "grp")
    first_user = lax.axis_index("grp") * owned
    observed = lax.dynamic_slice_in_dim(observed, first_user, owned, 0)
    right_side = lax.dynamic_slice_in_dim(right_side, first_user, owned, 0)
    local_gram = lax.dot_general(
        lax.dynamic_slice_in_dim(item_factors, offset, half, 1),
        item_factors,
        (((0,), (0,)), ((), ())),
        preferred_element_type=jnp.float32,
    )
    total_gram = lax.psum(local_gram, ("blk", "grp"))
    observed = observed + unobserved_weight * total_gram[None]
    owned_counts = lax.dynamic_slice_in_dim(counts, lax.axis_index("grp") * owned, owned, 0).astype(
        jnp.float32
    )
    rows_index = lax.broadcasted_iota(jnp.int32, (half, dim), 0) + offset
    cols_index = lax.broadcasted_iota(jnp.int32, (half, dim), 1)
    identity_half = (rows_index == cols_index).astype(jnp.float32)
    normal = observed + (regular_weight * owned_counts)[:, None, None] * identity_half[None]

    def squares(vector):
        return lax.psum(jnp.sum(vector * vector, axis=1), "rep")

    solution = jnp.zeros_like(right_side)
    residual = right_side
    direction = right_side
    norm_now = squares(residual)
    for turn in range(CG_STEPS):
        full_direction = lax.all_gather(direction, "rep", axis=1, tiled=True)
        image = jnp.einsum("ukl,ul->uk", normal, full_direction, precision=lax.Precision.HIGHEST)
        curvature_sum = lax.psum(jnp.sum(direction * image, axis=1), "rep")
        step_size = norm_now / (curvature_sum + epsilon)
        solution = solution + step_size[:, None] * direction
        residual = residual - step_size[:, None] * image
        norm_next = squares(residual)
        direction = residual + (norm_next / (norm_now + epsilon))[:, None] * direction
        norm_now = norm_next
    return solution


def solution(mesh):
    in_specs = (
        P(("parts", "blk", "grp"), None),
        P(("parts", "blk"), None, "grp"),
        P(("parts", "blk"), None, "grp"),
        P(("parts", "blk"), None, "grp"),
        P(("parts", "blk")),
    )
    out_specs = P(("parts", "blk", "grp"), "rep")
    return jax.shard_map(shards, mesh=mesh, in_specs=in_specs, out_specs=out_specs, check_vma=False)
```

profile of v0, /device:TPU:0, one launch (start us, length us, event | category | flops | bytes accessed | tf_op | source)
XLA Modules:
  0.0 116.0 jit_solution(14368306996446306912)
XLA Ops:
  6.5 0.8 copy.50
  7.6 0.7 copy-done.2
  8.2 0.7 copy-done.3
  9.0 0.6 copy-done.5
  9.6 0.6 fusion.26
  10.9 0.5 conditional.2
  11.0 0.3 fusion
  11.4 20.4 %while.19 = (s32[]{:T(128)}, bf16[128,128]{1,0:T(8,128)(2,1)S(1)}, f32[32,64,128]{2,1,0:T(8,128)S(1)}, f32[32,64]{1,0:T(8,128)S(1)}, s32[]{:T(128)}, /*index=5*/...) while((s32[]{:T(128)}, bf16[128,128]{1,0:T(8,128)(2,1)S(1)}, ...), condition=%wide.region_5.6_spmd, body=%wide.region_2.5_spmd.sunk | while | flops 68450320 | bytes 2589172 | solution.py:65
  11.4 3.0 %collective-permute-start = (bf16[128,128]{1,0:T(8,128)(2,1)S(1)}, bf16[128,128]{1,0:T(8,128)(2,1)S(1)}, u32[]{:S(2)}, u32[]{:S(2)}) collective-permute-start(bf16[128,128]{1,0:T(8,128)(2,1)S(1)} %get-tuple-element.458), channel_id=1, source_target_pairs={{12,0},{0,4},{4,8},{8,12},{13,1},{1,5},{5,9},{9,13},{14,2},{2,6},{... | collective-permute-start | bytes 98312 | tf_op jit(solution)/shard_map/while/body/eval_jaxpr/ppermute | solution.py:17
  14.4 0.6 dynamic_slice.95
  15.7 2.6 %collective-permute-done = bf16[128,128]{1,0:T(8,128)(2,1)S(1)} collective-permute-done((bf16[128,128]{1,0:T(8,128)(2,1)S(1)}, bf16[128,128]{1,0:T(8,128)(2,1)S(1)}, u32[]{:S(2)}, u32[]{:S(2)}) %collective-permute-start) | collective-permute-done | bytes 32800 | tf_op jit(solution)/shard_map/while/body/eval_jaxpr/ppermute | solution.py:17
  18.3 0.7 conditional.4
  18.5 0.3 convolution_add_fusion
  18.8 0.2 convolution_add_fusion.1
  19.1 0.7 dynamic_slice.95
  20.4 4.4 %collective-permute-done = bf16[128,128]{1,0:T(8,128)(2,1)S(1)} collective-permute-done((bf16[128,128]{1,0:T(8,128)(2,1)S(1)}, bf16[128,128]{1,0:T(8,128)(2,1)S(1)}, u32[]{:S(2)}, u32[]{:S(2)}) %collective-permute-start) | collective-permute-done | bytes 32800 | tf_op jit(solution)/shard_map/while/body/eval_jaxpr/ppermute | solution.py:17
  24.7 0.7 conditional.4
  24.9 0.3 convolution_add_fusion
  25.2 0.2 convolution_add_fusion.1
  25.5 0.7 dynamic_slice.95
  26.8 4.4 %collective-permute-done = bf16[128,128]{1,0:T(8,128)(2,1)S(1)} collective-permute-done((bf16[128,128]{1,0:T(8,128)(2,1)S(1)}, bf16[128,128]{1,0:T(8,128)(2,1)S(1)}, u32[]{:S(2)}, u32[]{:S(2)}) %collective-permute-start) | collective-permute-done | bytes 32800 | tf_op jit(solution)/shard_map/while/body/eval_jaxpr/ppermute | solution.py:17
  31.1 0.7 conditional.4
  31.3 0.3 convolution_add_fusion
  31.6 0.2 convolution_add_fusion.1
  31.8 1.0 copy-done
  32.9 7.5 %psum.77 = f32[32,64]{1,0:T(8,128)S(1)} all-reduce(f32[32,64]{1,0:T(8,128)S(1)} %get-tuple-element.306), channel_id=1, replica_groups=mesh['parts'=2,'blk'=4,'grp'=2,'rep'=2] {'grp'}, use_global_device_ids=true, to_apply=%region_6.7 | all-reduce | flops 2048 | bytes 16384 | tf_op jit(solution)/shard_map/psum | solution.py:68
  40.4 1.8 %all-gather = f32[2,64,16]{1,2,0:T(8,128)S(1)} all-gather(f32[1,64,16]{1,2,0:T(8,128)S(1)} %dynamic-slice_bitcast_fusion), channel_id=1, replica_groups=mesh['parts'=2,'blk'=4,'grp'=2,'rep'=2] {'rep'}, dimensions={0}, use_global_device_ids=true | all-gather | bytes 12288 | tf_op jit(solution)/shard_map/all_gather | solution.py:96
  42.3 0.2 fusion.27
  42.5 34.6 %psum.80 = f32[64,128]{1,0:T(8,128)S(1)} all-reduce(f32[64,128]{1,0:T(8,128)S(1)} %fusion.27), channel_id=1, replica_groups=mesh['parts'=2,'blk'=4,'grp'=2,'rep'=2] {'blk','grp'}, use_global_device_ids=true, to_apply=%region_10.11 | all-reduce | flops 8192 | bytes 65536 | tf_op jit(solution)/shard_map/psum | solution.py:78
  77.1 0.6 copy-done.6
  78.0 2.1 %fusion.25 = f32[16,1,64]{2,1,0:T(1,128)S(1)} fusion(f32[16,128,1]{1,2,0:T(1,128)S(1)} %bitcast.91, f32[32,64,128]{2,1,0:T(8,128)} %all-reduce.3.cloned.1.call-done, s32[]{:T(128)S(6)} %select_n.62, f32[64,128]{1,0:T(8,128)S(1)} %fusion.21, f32[16]{0:T(128)S(1)} %convert_multiply_fusion.2, f32[64,128]{1,0:T(8,128)S(1)} %broadcast_multiply_fusion), kind=kOutput, calls=%fused_computation.63 | convolution fusion | flops 1966080 | bytes 602180 | tf_op jit(solution)/shard_map/ukl,ul->uk/dot_general | solution.py:97
  80.2 2.5 %all-reduce = (f32[16]{0:T(128)S(1)}, f32[16]{0:T(128)S(1)}) all-reduce(f32[16]{0:T(128)S(1)} %get-tuple-element.351, f32[16]{0:T(128)S(1)} %get-tuple-element.350), channel_id=1, replica_groups=mesh['parts'=2,'blk'=4,'grp'=2,'rep'=2] {'rep'}, use_global_device_ids=true, to_apply=%region_8.9 | all-reduce | flops 32 | bytes 256 | tf_op jit(solution)/shard_map/psum | solution.py:89
  82.7 0.2 multiply_reduce_fusion.5
  82.9 2.5 %psum.82 = f32[16]{0:T(128)S(1)} all-reduce(f32[16]{0:T(128)S(1)} %get-tuple-element.374), channel_id=1, replica_groups=mesh['parts'=2,'blk'=4,'grp'=2,'rep'=2] {'rep'}, use_global_device_ids=true, to_apply=%region_14.15 | all-reduce | flops 16 | bytes 128 | tf_op jit(solution)/shard_map/psum | solution.py:89
  85.5 1.8 %all-gather.1 = f32[2,64,16]{1,2,0:T(8,128)S(1)} all-gather(f32[1,64,16]{1,2,0:T(8,128)S(1)} %bitcast.81), channel_id=1, replica_groups=mesh['parts'=2,'blk'=4,'grp'=2,'rep'=2] {'rep'}, dimensions={0}, use_global_device_ids=true | all-gather | bytes 12288 | tf_op jit(solution)/shard_map/all_gather | solution.py:96
  87.4 2.0 %fusion.24 = f32[16,1,64]{2,1,0:T(1,128)S(1)} fusion(f32[16,128,1]{1,2,0:T(1,128)S(1)} %bitcast.93, f32[32,64,128]{2,1,0:T(8,128)} %all-reduce.3.cloned.1.call-done, s32[]{:T(128)S(6)} %select_n.62, f32[64,128]{1,0:T(8,128)S(1)} %fusion.21, f32[16]{0:T(128)S(1)} %convert_multiply_fusion.2, f32[64,128]{1,0:T(8,128)S(1)} %broadcast_multiply_fusion), kind=kOutput, calls=%fused_computation.62 | convolution fusion | flops 1966080 | bytes 602180 | tf_op jit(solution)/shard_map/ukl,ul->uk/dot_general | solution.py:97
  89.5 2.5 %psum.83 = f32[16]{0:T(128)S(1)} all-reduce(f32[16]{0:T(128)S(1)} %multiply_reduce_fusion.4), channel_id=1, replica_groups=mesh['parts'=2,'blk'=4,'grp'=2,'rep'=2] {'rep'}, use_global_device_ids=true, to_apply=%region_16.17 | all-reduce | flops 16 | bytes 128 | tf_op jit(solution)/shard_map/psum | solution.py:98
  92.0 0.2 multiply_reduce_fusion.3
  92.2 2.5 %psum.84 = f32[16]{0:T(128)S(1)} all-reduce(f32[16]{0:T(128)S(1)} %get-tuple-element.372), channel_id=1, replica_groups=mesh['parts'=2,'blk'=4,'grp'=2,'rep'=2] {'rep'}, use_global_device_ids=true, to_apply=%region_18.19 | all-reduce | flops 16 | bytes 128 | tf_op jit(solution)/shard_map/psum | solution.py:89
  94.7 1.8 %all-gather.2 = f32[2,64,16]{1,2,0:T(8,128)S(1)} all-gather(f32[1,64,16]{1,2,0:T(8,128)S(1)} %bitcast.82), channel_id=1, replica_groups=mesh['parts'=2,'blk'=4,'grp'=2,'rep'=2] {'rep'}, dimensions={0}, use_global_device_ids=true | all-gather | bytes 12288 | tf_op jit(solution)/shard_map/all_gather | solution.py:96
  96.6 1.0 fusion.23
  97.8 2.5 %psum.85 = f32[16]{0:T(128)S(1)} all-reduce(f32[16]{0:T(128)S(1)} %multiply_reduce_fusion.2), channel_id=1, replica_groups=mesh['parts'=2,'blk'=4,'grp'=2,'rep'=2] {'rep'}, use_global_device_ids=true, to_apply=%region_20.21 | all-reduce | flops 16 | bytes 128 | tf_op jit(solution)/shard_map/psum | solution.py:98
  100.2 0.2 multiply_reduce_fusion.1
  100.4 2.5 %psum.86 = f32[16]{0:T(128)S(1)} all-reduce(f32[16]{0:T(128)S(1)} %multiply_reduce_fusion.1), channel_id=1, replica_groups=mesh['parts'=2,'blk'=4,'grp'=2,'rep'=2] {'rep'}, use_global_device_ids=true, to_apply=%region_22.23 | all-reduce | flops 16 | bytes 128 | tf_op jit(solution)/shard_map/psum | solution.py:89
  103.0 1.8 %all-gather.3 = f32[2,64,16]{1,2,0:T(8,128)S(1)} all-gather(f32[1,64,16]{1,2,0:T(8,128)S(1)} %bitcast.83), channel_id=1, replica_groups=mesh['parts'=2,'blk'=4,'grp'=2,'rep'=2] {'rep'}, dimensions={0}, use_global_device_ids=true | all-gather | bytes 12288 | tf_op jit(solution)/shard_map/all_gather | solution.py:96
  104.9 1.0 fusion.22
  106.0 2.5 %psum.87 = f32[16]{0:T(128)S(1)} all-reduce(f32[16]{0:T(128)S(1)} %multiply_reduce_fusion), channel_id=1, replica_groups=mesh['parts'=2,'blk'=4,'grp'=2,'rep'=2] {'rep'}, use_global_device_ids=true, to_apply=%region_24.25 | all-reduce | flops 16 | bytes 128 | tf_op jit(solution)/shard_map/psum | solution.py:98
  108.5 0.7 multiply_add_fusion.1
  (62 shorter events, 2.2 us)
Async XLA Ops:
  6.5 71.4 %all-reduce.3.cloned.1.call-start = ((), (), s32[]{:S(2)}) async-start(), calls=%async_computation | async-start | bytes 2097152 | tf_op jit(solution)/shard_map/psum | solution.py:68
  6.5 0.8 copy-start.1
  7.5 0.8 copy-start.2
  8.2 0.8 copy-start.3
  9.0 0.7 copy-start.5
  11.4 6.9 %collective-permute-start = (bf16[128,128]{1,0:T(8,128)(2,1)S(1)}, bf16[128,128]{1,0:T(8,128)(2,1)S(1)}, u32[]{:S(2)}, u32[]{:S(2)}) collective-permute-start(bf16[128,128]{1,0:T(8,128)(2,1)S(1)} %get-tuple-element.458), channel_id=1, source_target_pairs={{12,0},{0,4},{4,8},{8,12},{13,1},{1,5},{5,9},{9,13},{14,2},{2,6},{... | collective-permute-start | bytes 98312 | tf_op jit(solution)/shard_map/while/body/eval_jaxpr/ppermute | solution.py:17
  19.0 5.7 %collective-permute-start = (bf16[128,128]{1,0:T(8,128)(2,1)S(1)}, bf16[128,128]{1,0:T(8,128)(2,1)S(1)}, u32[]{:S(2)}, u32[]{:S(2)}) collective-permute-start(bf16[128,128]{1,0:T(8,128)(2,1)S(1)} %get-tuple-element.458), channel_id=1, source_target_pairs={{12,0},{0,4},{4,8},{8,12},{13,1},{1,5},{5,9},{9,13},{14,2},{2,6},{... | collective-permute-start | bytes 98312 | tf_op jit(solution)/shard_map/while/body/eval_jaxpr/ppermute | solution.py:17
  25.4 5.7 %collective-permute-start = (bf16[128,128]{1,0:T(8,128)(2,1)S(1)}, bf16[128,128]{1,0:T(8,128)(2,1)S(1)}, u32[]{:S(2)}, u32[]{:S(2)}) collective-permute-start(bf16[128,128]{1,0:T(8,128)(2,1)S(1)} %get-tuple-element.458), channel_id=1, source_target_pairs={{12,0},{0,4},{4,8},{8,12},{13,1},{1,5},{5,9},{9,13},{14,2},{2,6},{... | collective-permute-start | bytes 98312 | tf_op jit(solution)/shard_map/while/body/eval_jaxpr/ppermute | solution.py:17
  31.8 1.0 copy-start
  77.1 0.7 copy-start.6
  78.0 18.7 %copy-start.4 = (f32[32,64,128]{2,1,0:T(8,128)S(1)}, f32[32,64,128]{2,1,0:T(8,128)}, u32[]{:S(2)}) copy-start(f32[32,64,128]{2,1,0:T(8,128)} %all-reduce.3.cloned.1.call-done) | copy-start | bytes 3145732
Sparse Core Ops, SparseCore 0:
  33.0 37.9 all-reduce.2
where the time goes:
time: 116 us
  blocking collectives  66.7 us (58%)
  between operations  14.2 us (12%)
  waiting for transfers between devices  11.4 us (10%)
  matrix products  8.28 us (7%)
  local copies, waits for them, and re-layouts  7.3 us (6%)
  starting transfers between devices  3.07 us (3%)
  other arithmetic  3.03 us (3%)
  loops' own time  2.08 us (2%)
    psum x1, blocking collectives, shards(): total_gram = lax.psum(local_gram, ('blk', 'grp'))  34.6 us
    ppermute x3, waiting for transfers between devices, from_behind(): return lax.ppermute(block, axis, route)  11.4 us
    psum x4, blocking collectives, squares(): return lax.psum(jnp.sum(vector * vector, axis=1), 'rep')  9.87 us
    psum x1, blocking collectives, shards(): observed, right_side = lax.psum((observed, right_side), 'grp')  7.54 us
    psum x3, blocking collectives, shards(): curvature_sum = lax.psum(jnp.sum(direction * image, axis=1), 'rep')  7.41 us
    all_gather x4, blocking collectives, shards(): full_direction = lax.all_gather(direction, 'rep', axis=1, tiled=True)  7.22 us
    dot_general x4, matrix products, shards(): jnp.einsum('ukl,ul->uk', normal, full_direction, precision=lax.Precision....  6.15 us
    unnamed x22, local copies, waits for them, and re-layouts  5.07 us
  transfers between devices with their start and end apart: 4, of which 3 were waited for; matrix products, arithmetic and copies ran while one was open for 2% of the time, Pallas kernels for 0%

commit v1 on v0

v1 whole, which is shorter than its diff:
```python
import functools

import jax
import jax.numpy as jnp
from jax import lax
from jax.experimental import pallas as pl
from jax.experimental.pallas import tpu as pltpu
from jax.sharding import PartitionSpec as P

CG_STEPS = 4

unobserved_weight = 0.25
regular_weight = 0.002
epsilon = 1e-06


def halves(value):
    high = value.astype(jnp.bfloat16)
    low = (value - high.astype(jnp.float32)).astype(jnp.bfloat16)
    return jnp.concatenate([high, low], axis=0)


def joined(value, rows):
    return value[:rows] + value[rows:]


def solve_kernel(half, offset_ref, factors_ref, pair_ref, counts_ref, out_ref):
    factors = factors_ref[...]
    weights = pair_ref[0].astype(jnp.float32) + unobserved_weight
    rows = weights.shape[0]
    ridge = regular_weight * counts_ref[...].astype(jnp.float32)
    right_side = jnp.dot(pair_ref[1], factors, preferred_element_type=jnp.float32)

    def project(direction):
        return joined(
            lax.dot_general(
                halves(direction),
                factors,
                (((1,), (1,)), ((), ())),
                preferred_element_type=jnp.float32,
            ),
            rows,
        )

    def back(values):
        return joined(
            jnp.dot(halves(values), factors, preferred_element_type=jnp.float32),
            rows,
        )

    total = jnp.zeros_like(right_side)
    residual = right_side
    direction = right_side
    norm_now = jnp.sum(residual * residual, axis=1, keepdims=True)
    for turn in range(CG_STEPS):
        image = back(project(direction) * weights) + ridge * direction
        step_size = norm_now / (jnp.sum(direction * image, axis=1, keepdims=True) + epsilon)
        total = total + step_size * direction
        if turn == CG_STEPS - 1:
            break
        residual = residual - step_size * image
        norm_next = jnp.sum(residual * residual, axis=1, keepdims=True)
        direction = residual + (norm_next / (norm_now + epsilon)) * direction
        norm_now = norm_next
    dim = total.shape[1]
    if half == dim:
        out_ref[...] = total
    else:
        core = offset_ref[0]
        chosen = total[:, :half]
        for other in range(1, dim // half):
            chosen = jnp.where(core == other, total[:, other * half : (other + 1) * half], chosen)
        out_ref[...] = chosen


def shards(item_factors, confidence, ratings, pattern, counts):
    tile_items, dim = item_factors.shape
    groups = lax.axis_size("grp")
    group = lax.axis_index("grp")
    cores = lax.axis_size("rep")
    core = lax.axis_index("rep")
    half = dim // cores
    users = confidence.shape[0]
    owned = users // groups
    cycle_size = confidence.shape[1]

    factors = lax.all_gather(item_factors, ("grp", "blk"), axis=0, tiled=True)

    flags = (pattern[0, :, 0] != 0)[None, :, None]
    weight = jnp.where(flags, confidence, jnp.zeros_like(confidence))
    paired = (weight.astype(jnp.float32) * ratings.astype(jnp.float32)).astype(jnp.bfloat16)
    pair = jnp.stack([weight, paired]).reshape(2, groups, owned, cycle_size * tile_items)
    pieces = []
    for distance in range(groups):
        part = lax.dynamic_index_in_dim(pair, (group + distance) % groups, 1, keepdims=False)
        if distance:
            part = lax.ppermute(
                part, "grp", [(i, (i + distance) % groups) for i in range(groups)]
            )
        pieces.append(part)
    received = jnp.stack(pieces)
    order = (group - jnp.arange(groups)) % groups
    received = received[order]
    all_pair = jnp.moveaxis(received, 0, 2).reshape(2, owned, -1)
    owned_counts = lax.dynamic_slice_in_dim(counts, group * owned, owned, 0)[:, None]
    return pl.pallas_call(
        functools.partial(solve_kernel, half),
        out_shape=jax.ShapeDtypeStruct((owned, half), jnp.float32),
        in_specs=[pl.BlockSpec(memory_space=pltpu.SMEM)]
        + [pl.BlockSpec(memory_space=pltpu.VMEM)] * 3,
        out_specs=pl.BlockSpec(memory_space=pltpu.VMEM),
        compiler_params=pltpu.CompilerParams(vmem_limit_bytes=48 * 1024 * 1024),
    )(core[None].astype(jnp.int32), factors, all_pair, owned_counts)


def solution(mesh):
    in_specs = (
        P(("parts", "blk", "grp"), None),
        P(("parts", "blk"), None, "grp"),
        P(("parts", "blk"), None, "grp"),
        P(("parts", "blk"), None, "grp"),
        P(("parts", "blk")),
    )
    out_specs = P(("parts", "blk", "grp"), "rep")
    return jax.shard_map(shards, mesh=mesh, in_specs=in_specs, out_specs=out_specs, check_vma=False)
```

time: 116 us -> 39.6 us (0.34)
  blocking collectives: 66.7 us -> 31.2 us
  between operations: 14.2 us -> 0.08 us
  waiting for transfers between devices: 11.4 us -> 0.01 us
  matrix products: 8.28 us -> 0 us
  local copies, waits for them, and re-layouts: 7.3 us -> 1.55 us
  Pallas kernels: 0 us -> 2.64 us
  other arithmetic: 3.03 us -> 0.89 us
  loops' own time: 2.08 us -> 0 us
    psum x9 -> x0, blocking collectives: 59.5 us -> none  [the longest x1 34.6 us: shards(): total_gram = lax.psum(local_gram, ('blk', 'grp'))]
    all_gather x4 -> x1, blocking collectives: 7.22 us -> 31.2 us  [shards(): factors = lax.all_gather(item_factors, ('grp', 'blk'), axis=0, tiled=True)]
    ppermute x3 -> x1, waiting for transfers between devices: 11.4 us -> 0.01 us  [shards(): lax.ppermute(part, 'grp', [(i, (i + distance) % groups) for i in range(gr...]
    dot_general x13 -> x0, matrix products: 8.28 us -> none  [the longest x4 6.15 us: shards(): jnp.einsum('ukl,ul->uk', normal, full_direction, precision=lax.Precision....]
    unnamed x22 -> x8, local copies, waits for them, and re-layouts: 5.07 us -> 0.79 us
    pallas_call x0 -> x1, Pallas kernels: none -> 2.64 us  [shards(): pl.pallas_call(functools.partial(solve_kernel, half), out_shape=jax.Shape...]
    another operation x5 -> x0, loops' own time: 2.08 us -> none  [the longest x1 1.99 us: shards(): lax.fori_loop(1, cycle_size, single_turn, (item_factors, state))]
    dynamic_slice x3 -> x0, local copies, waits for them, and re-layouts: 1.95 us -> none  [accumulate(): flag = lax.dynamic_index_in_dim(flags, source, 0, keepdims=False)]
  transfers between devices with their start and end apart: 4 -> 1, of which waited for: 3 -> 0; matrix products, arithmetic and copies ran while one was open for 2% -> 0% of each run, Pallas kernels for 0% -> 0%
where the time goes in v1:
time: 39.6 us; the launch traced here: 39.3 us
  blocking collectives  31.2 us (79%)
  starting transfers between devices  3 us (8%)
  Pallas kernels  2.64 us (7%)
  local copies, waits for them, and re-layouts  1.55 us (4%)
  other arithmetic  0.89 us (2%)
    all_gather x1, blocking collectives, shards(): factors = lax.all_gather(item_factors, ('grp', 'blk'), axis=0, tiled=True)  31.2 us
    ppermute x1, starting transfers between devices, shards(): lax.ppermute(part, 'grp', [(i, (i + distance) % groups) for i in range(gr...  3 us
    pallas_call x1, Pallas kernels, shards(): pl.pallas_call(functools.partial(solve_kernel, half), out_shape=jax.Shape...  2.64 us
    convert_element_type x1, other arithmetic, shards(): (weight.astype(jnp.float32) * ratings.astype(jnp.float32)).astype(jnp.bfl...  0.85 us
  transfers between devices with their start and end apart: 1, of which 0 were waited for; matrix products, arithmetic and copies ran while one was open for 0% of the time, Pallas kernels for 0%

profile of v1, /device:TPU:0, one launch (start us, length us, event | category | flops | bytes accessed | tf_op | source)
XLA Modules:
  0.0 39.3 jit_solution(10995988822029932748)
XLA Ops:
  0.0 0.0 copy-start
  0.0 0.0 copy-start.2
  0.0 0.0 copy-start.3
  0.0 0.7 %copy-done.3 = s32[1,4,1]{1,2,0:T(1,128)S(1)} copy-done((s32[1,4,1]{1,2,0:T(1,128)S(1)}, s32[1,4,1]{1,2,0:T(1,128)}, u32[]{:S(2)}) %copy-start.3) | copy-done | bytes 40
  0.7 0.1 copy-done.2
  0.8 0.8 %multiply_convert_fusion = (bf16[32,4,128]{2,1,0:T(4,128)(2,1)S(1)}, bf16[32,4,128]{2,1,0:T(4,128)(2,1)S(1)}) fusion(bf16[32,4,128]{2,1,0:T(4,128)(2,1)S(1)} %copy-done.2, bf16[32,4,128]{2,1,0:T(4,128)(2,1)} %param.6, pred[4]{0:T(512)(128)(4,1)S(1)} %compare_bitcast_fusion), kind=kLoop, calls=%fused_computation.6 | loop fusion | flops 81920 | bytes 131076 | tf_op jit(solution)/shard_map/convert_element_type | solution.py:91
  1.7 0.0 copy-start.1
  1.7 3.0 %collective-permute-start = (bf16[2,16,512]{2,1,0:T(8,128)(2,1)S(1)}, bf16[2,16,512]{2,1,0:T(8,128)(2,1)S(1)}, u32[]{:S(2)}, u32[]{:S(2)}) collective-permute-start(bf16[2,16,512]{2,1,0:T(8,128)(2,1)S(1)} %get-tuple-element.8), channel_id=1, source_target_pairs={{0,2},{2,0},{1,3},{3,1},{4,6},{6,4},{5,7},{7,5},{8,10},{10,8},{9,1... | collective-permute-start | bytes 98312 | tf_op jit(solution)/shard_map/ppermute | solution.py:97
  4.8 0.0 copy-done.1
  4.8 31.2 %all_gather.3.factors_ref = bf16[1024,128]{1,0:T(8,128)(2,1)S(1)} all-gather(bf16[128,128]{1,0:T(8,128)(2,1)S(1)} %copy-done.1), channel_id=1, replica_groups=mesh['parts'=2,'blk'=4,'grp'=2,'rep'=2] {'grp','blk'}, dimensions={0}, use_global_device_ids=true | all-gather | bytes 294912 | tf_op jit(solution)/shard_map/all_gather | solution.py:87
  35.9 0.0 copy-done
  35.9 0.1 dynamic-slice_bitcast_fusion
  36.0 0.1 copy.10.counts_ref
  36.1 0.0 collective-permute-done
  36.1 0.6 %gather_fusion = bf16[2,2,16,512]{3,2,1,0:T(8,128)(2,1)S(1)} fusion(bf16[2,2,16,512]{3,2,1,0:T(8,128)(2,1)S(1)} %pad_maximum_fusion, s32[1024]{0:T(1024)S(1)} %pad_clamp_fusion), kind=kCustom, calls=%fused_computation | custom fusion | bytes 131080 | tf_op jit(solution)/shard_map/gather | solution.py:103
  36.7 2.6 %shard_map.55 = f32[16,64]{1,0:T(8,128)} custom-call(s32[1]{0:T(128)} %bitcast.offset_ref, bf16[1024,128]{1,0:T(8,128)(2,1)S(1)} %all_gather.3.factors_ref, bf16[2,16,1024]{2,1,0:T(8,128)(2,1)S(1)} %bitcast.17, s32[16,1]{1,0:T(8,128)S(1)} %copy.10.counts_ref), custom_call_target="tpu_custom_call" | custom-call | tf_op jit(solution)/shard_map/pallas_call | solution.py:106
  (8 shorter events, 0.1 us)
Async XLA Ops:
  0.0 35.9 %copy-start = (s32[32]{0:T(128)S(1)}, s32[32]{0:T(128)}, u32[]{:S(2)}) copy-start(s32[32]{0:T(128)} %param.9) | copy-start | bytes 388
  0.0 0.8 %copy-start.2 = (bf16[32,4,128]{2,1,0:T(4,128)(2,1)S(1)}, bf16[32,4,128]{2,1,0:T(4,128)(2,1)}, u32[]{:S(2)}) copy-start(bf16[32,4,128]{2,1,0:T(4,128)(2,1)} %param.7) | copy-start | bytes 98308
  0.0 0.7 %copy-start.3 = (s32[1,4,1]{1,2,0:T(1,128)S(1)}, s32[1,4,1]{1,2,0:T(1,128)}, u32[]{:S(2)}) copy-start(s32[1,4,1]{1,2,0:T(1,128)} %param.8) | copy-start | bytes 52
  1.7 3.1 %copy-start.1 = (bf16[128,128]{1,0:T(8,128)(2,1)S(1)}, bf16[128,128]{1,0:T(8,128)(2,1)}, u32[]{:S(2)}) copy-start(bf16[128,128]{1,0:T(8,128)(2,1)} %param.5) | copy-start | bytes 98308
  1.7 34.4 %collective-permute-start = (bf16[2,16,512]{2,1,0:T(8,128)(2,1)S(1)}, bf16[2,16,512]{2,1,0:T(8,128)(2,1)S(1)}, u32[]{:S(2)}, u32[]{:S(2)}) collective-permute-start(bf16[2,16,512]{2,1,0:T(8,128)(2,1)S(1)} %get-tuple-element.8), channel_id=1, source_target_pairs={{0,2},{2,0},{1,3},{3,1},{4,6},{6,4},{5,7},{7,5},{8,10},{10,8},{9,1... | collective-permute-start | bytes 98312 | tf_op jit(solution)/shard_map/ppermute | solution.py:97

commit v2 on v1

--- a/solution.py
+++ b/solution.py
@@ -13,6 +13,40 @@
 regular_weight = 0.002
 epsilon = 1e-06
 
+PLACE = ("blk", "grp", "rep")
+LINE = (0, 1, 2, 3)
+FOLDED = (0, 1, 3, 2)
+EXCHANGES = (
+    ((LINE, 2, 0), (LINE, 1, 1)),
+    ((LINE, 0, 1), (LINE, 0, 1)),
+    ((LINE, 1, 0), (LINE, 3, 1)),
+    ((LINE, 3, 0), (LINE, 2, 1)),
+)
+
+
+def stepped(order, position, steps):
+    return order[(order.index(position) + steps) % len(order)]
+
+
+def exchange_route(rules):
+    route = []
+    for core, (order, steps, other) in enumerate(rules):
+        for position in range(4):
+            for group in range(2):
+                target = stepped(order, position, steps)
+                route.append(
+                    ((position * 2 + group) * 2 + core, (target * 2 + (group ^ other)) * 2 + core)
+                )
+    return route
+
+
+def source_slot(rule, position):
+    order, steps, other = rule
+    slot = jnp.int32(0)
+    for target in range(4):
+        slot = jnp.where(position == target, 4 * other + stepped(order, target, -steps), slot)
+    return slot
+
 
 def halves(value):
     high = value.astype(jnp.bfloat16)
@@ -24,12 +58,10 @@
     return value[:rows] + value[rows:]
 
 
-def solve_kernel(half, offset_ref, factors_ref, pair_ref, counts_ref, out_ref):
-    factors = factors_ref[...]
-    weights = pair_ref[0].astype(jnp.float32) + unobserved_weight
-    rows = weights.shape[0]
-    ridge = regular_weight * counts_ref[...].astype(jnp.float32)
-    right_side = jnp.dot(pair_ref[1], factors, preferred_element_type=jnp.float32)
+def conjugate_gradient(factors, weighted, paired, ridge):
+    rows = weighted.shape[0]
+    weights = weighted + unobserved_weight
+    right_side = jnp.dot(paired, factors, preferred_element_type=jnp.float32)
 
     def project(direction):
         return joined(
@@ -62,27 +94,106 @@
         norm_next = jnp.sum(residual * residual, axis=1, keepdims=True)
         direction = residual + (norm_next / (norm_now + epsilon)) * direction
         norm_now = norm_next
-    dim = total.shape[1]
-    if half == dim:
-        out_ref[...] = total
-    else:
-        core = offset_ref[0]
-        chosen = total[:, :half]
-        for other in range(1, dim // half):
-            chosen = jnp.where(core == other, total[:, other * half : (other + 1) * half], chosen)
-        out_ref[...] = chosen
-
-
-def shards(item_factors, confidence, ratings, pattern, counts):
+    return total
+
+
+def columns_of(total, core, half):
+    chosen = total[:, :half]
+    for other in range(1, total.shape[1] // half):
+        chosen = jnp.where(core == other, total[:, other * half : (other + 1) * half], chosen)
+    return chosen
+
+
+def pair_kernel(flags_ref, confidence_ref, ratings_ref, mine_ref, theirs_ref):
+    group = lax.axis_index("grp")
+    users, cycle_size, tile_items = confidence_ref.shape
+    owned = users // 2
+    weight = confidence_ref[...].astype(jnp.float32)
+    rating = ratings_ref[...].astype(jnp.float32)
+    for source in range(cycle_size):
+        flag = flags_ref[source] != 0
+        masked = jnp.where(flag, weight[:, source, :], 0.0)
+        product = masked * rating[:, source, :]
+        for kind, value in enumerate((masked, product)):
+            value = value.astype(jnp.bfloat16)
+            first, second = value[:owned], value[owned:]
+            mine_ref[kind, source] = jnp.where(group == 0, first, second)
+            theirs_ref[kind, source] = jnp.where(group == 0, second, first)
+
+
+def chip_kernel(*refs):
+    own_ref, *block_refs, mine_ref, theirs_ref, counts_ref, out_ref, held = refs
+    position = lax.axis_index("blk")
+    core = lax.axis_index("rep")
+    cycle_size, dim = mine_ref.shape[1], own_ref.shape[1]
+    held[position] = own_ref[...]
+    direct = block_refs[: len(EXCHANGES)]
+    passed = list(block_refs[len(EXCHANGES) :])
+    for rules, block_ref in zip(EXCHANGES, direct):
+        slots = [source_slot(rule, position) for rule in rules]
+        held[jnp.where(core == 0, slots[0], slots[1])] = block_ref[...]
+        if rules[0] != rules[1]:
+            held[jnp.where(core == 0, slots[1], slots[0])] = passed.pop(0)[...]
+    factors = held[...].reshape(-1, dim)
+    blocks = [ref.at[:, source] for ref in (mine_ref, theirs_ref) for source in range(cycle_size)]
+    weighted = jnp.concatenate([block[0] for block in blocks], axis=1).astype(jnp.float32)
+    paired = jnp.concatenate([block[1] for block in blocks], axis=1)
+    ridge = regular_weight * counts_ref[...].astype(jnp.float32)
+    total = conjugate_gradient(factors, weighted, paired, ridge)
+    out_ref[...] = columns_of(total, core, out_ref.shape[1])
+
+
+VMEM = pl.BlockSpec(memory_space=pltpu.VMEM)
+SMEM = pl.BlockSpec(memory_space=pltpu.SMEM)
+
+
+def chip_shards(item_factors, confidence, ratings, pattern, counts):
+    tile_items, dim = item_factors.shape
+    users, cycle_size = confidence.shape[:2]
+    owned = users // 2
+    group = lax.axis_index("grp")
+    swap = [(0, 1), (1, 0)]
+    direct = [lax.ppermute(item_factors, PLACE, exchange_route(rules)) for rules in EXCHANGES]
+    passed = [
+        lax.ppermute(block, "rep", swap)
+        for rules, block in zip(EXCHANGES, direct)
+        if rules[0] != rules[1]
+    ]
+    half_shape = jax.ShapeDtypeStruct((2, cycle_size, owned, tile_items), jnp.bfloat16)
+    mine, theirs = pl.pallas_call(
+        pair_kernel,
+        out_shape=(half_shape, half_shape),
+        in_specs=[SMEM, VMEM, VMEM],
+        out_specs=(VMEM, VMEM),
+        compiler_params=pltpu.CompilerParams(vmem_limit_bytes=8 * 1024 * 1024),
+    )(pattern[0, :, 0], confidence, ratings)
+    theirs = lax.ppermute(theirs, "grp", swap)
+    owned_counts = lax.dynamic_slice_in_dim(counts, group * owned, owned, 0)[:, None]
+    return pl.pallas_call(
+        chip_kernel,
+        out_shape=jax.ShapeDtypeStruct((owned, dim // 2), jnp.float32),
+        in_specs=[VMEM] * (4 + len(direct) + len(passed)),
+        out_specs=VMEM,
+        scratch_shapes=[pltpu.VMEM((2 * cycle_size, tile_items, dim), jnp.bfloat16)],
+        compiler_params=pltpu.CompilerParams(vmem_limit_bytes=8 * 1024 * 1024),
+    )(item_factors, *direct, *passed, mine, theirs, owned_counts)
+
+
+def gathered_kernel(factors_ref, pair_ref, counts_ref, out_ref):
+    ridge = regular_weight * counts_ref[...].astype(jnp.float32)
+    total = conjugate_gradient(
+        factors_ref[...], pair_ref[0].astype(jnp.float32), pair_ref[1], ridge
+    )
+    out_ref[...] = columns_of(total, lax.axis_index("rep"), out_ref.shape[1])
+
+
+def gathered_shards(item_factors, confidence, ratings, pattern, counts):
     tile_items, dim = item_factors.shape
     groups = lax.axis_size("grp")
     group = lax.axis_index("grp")
-    cores = lax.axis_size("rep")
-    core = lax.axis_index("rep")
-    half = dim // cores
-    users = confidence.shape[0]
+    half = dim // lax.axis_size("rep")
+    users, cycle_size = confidence.shape[:2]
     owned = users // groups
-    cycle_size = confidence.shape[1]
 
     factors = lax.all_gather(item_factors, ("grp", "blk"), axis=0, tiled=True)
 
@@ -98,19 +209,16 @@
                 part, "grp", [(i, (i + distance) % groups) for i in range(groups)]
             )
         pieces.append(part)
-    received = jnp.stack(pieces)
-    order = (group - jnp.arange(groups)) % groups
-    received = received[order]
+    received = jnp.stack(pieces)[(group - jnp.arange(groups)) % groups]
     all_pair = jnp.moveaxis(received, 0, 2).reshape(2, owned, -1)
     owned_counts = lax.dynamic_slice_in_dim(counts, group * owned, owned, 0)[:, None]
     return pl.pallas_call(
-        functools.partial(solve_kernel, half),
+        gathered_kernel,
         out_shape=jax.ShapeDtypeStruct((owned, half), jnp.float32),
-        in_specs=[pl.BlockSpec(memory_space=pltpu.SMEM)]
-        + [pl.BlockSpec(memory_space=pltpu.VMEM)] * 3,
-        out_specs=pl.BlockSpec(memory_space=pltpu.VMEM),
+        in_specs=[VMEM] * 3,
+        out_specs=VMEM,
         compiler_params=pltpu.CompilerParams(vmem_limit_bytes=48 * 1024 * 1024),
-    )(core[None].astype(jnp.int32), factors, all_pair, owned_counts)
+    )(factors, all_pair, owned_counts)
 
 
 def solution(mesh):
@@ -122,4 +230,6 @@
         P(("parts", "blk")),
     )
     out_specs = P(("parts", "blk", "grp"), "rep")
+    sizes = tuple(mesh.shape[axis] for axis in PLACE)
+    shards = chip_shards if sizes == (4, 2, 2) else gathered_shards
     return jax.shard_map(shards, mesh=mesh, in_specs=in_specs, out_specs=out_specs, check_vma=False)

time: 39.6 us -> 18.6 us (0.47)
  blocking collectives: 31.2 us -> 0 us
  starting transfers between devices: 3 us -> 10.5 us
  waiting for transfers between devices: 0.01 us -> 2.64 us
  other arithmetic: 0.89 us -> 0 us
  Pallas kernels: 2.64 us -> 3.44 us
    all_gather x1 -> x0, blocking collectives: 31.2 us -> none  [shards(): factors = lax.all_gather(item_factors, ('grp', 'blk'), axis=0, tiled=True)]
    ppermute x1 -> x8, starting transfers between devices: 3 us -> 10.5 us  [the longest x4 9.35 us: chip_shards(): lax.ppermute(item_factors, PLACE, exchange_route(rules))]
    ppermute x1 -> x8, waiting for transfers between devices: 0.01 us -> 2.64 us  [the longest x1 2.62 us: chip_shards(): theirs = lax.ppermute(theirs, 'grp', swap)]
    convert_element_type x1 -> x0, other arithmetic: 0.85 us -> none  [shards(): (weight.astype(jnp.float32) * ratings.astype(jnp.float32)).astype(jnp.bfl...]
    pallas_call x1 -> x2, Pallas kernels: 2.64 us -> 3.44 us  [the longest x1 2.67 us: chip_shards(): pl.pallas_call(chip_kernel, out_shape=jax.ShapeDtypeStruct((owned, dim //...]
    unnamed x8 -> x10, local copies, waits for them, and re-layouts: 0.79 us -> 1.53 us
    gather x1 -> x0, local copies, waits for them, and re-layouts: 0.55 us -> none  [shards(): received = received[order]]
  transfers between devices with their start and end apart: 1 -> 8, of which waited for: 0 -> 1; matrix products, arithmetic and copies ran while one was open for 0% -> 1% of each run, Pallas kernels for 0% -> 4%
where the time goes in v2:
time: 18.6 us; the launch traced here: 18.3 us
  starting transfers between devices  10.5 us (56%)
  Pallas kernels  3.44 us (18%)
  waiting for transfers between devices  2.64 us (14%)
  local copies, waits for them, and re-layouts  1.69 us (9%)
    ppermute x4, starting transfers between devices, chip_shards(): lax.ppermute(item_factors, PLACE, exchange_route(rules))  9.35 us
    pallas_call x1, Pallas kernels, chip_shards(): pl.pallas_call(chip_kernel, out_shape=jax.ShapeDtypeStruct((owned, dim //...  2.67 us
    ppermute x1, waiting for transfers between devices, chip_shards(): theirs = lax.ppermute(theirs, 'grp', swap)  2.62 us
    unnamed x10, local copies, waits for them, and re-layouts  1.53 us
    pallas_call x1, Pallas kernels, chip_shards(): pl.pallas_call(pair_kernel, out_shape=(half_shape, half_shape), in_specs=...  0.76 us
    ppermute x1, starting transfers between devices, chip_shards(): theirs = lax.ppermute(theirs, 'grp', swap)  0.6 us
    ppermute x3, starting transfers between devices, chip_shards(): lax.ppermute(block, 'rep', swap)  0.58 us
  transfers between devices with their start and end apart: 8, of which 1 were waited for; matrix products, arithmetic and copies ran while one was open for 1% of the time, Pallas kernels for 4%

profile of v2, /device:TPU:0, one launch (start us, length us, event | category | flops | bytes accessed | tf_op | source)
XLA Modules:
  0.0 18.3 jit_solution(10386750761153505723)
XLA Ops:
  0.0 0.0 copy-start
  0.0 0.0 copy-start.4
  0.0 4.0 %collective-permute-start = (bf16[128,128]{1,0:T(8,128)(2,1)}, bf16[128,128]{1,0:T(8,128)(2,1)S(1)}, u32[]{:S(2)}, u32[]{:S(2)}) collective-permute-start(bf16[128,128]{1,0:T(8,128)(2,1)} %refs_0_.1), channel_id=1, source_target_pairs={{0,8},{2,10},{4,12},{6,14},{8,0},{10,2},{12,4},{14,6},{1,7},{3,5},... | collective-permute-start | bytes 98312 | tf_op jit(solution)/shard_map/ppermute | solution.py:156
  4.0 1.6 %collective-permute-start.2 = (bf16[128,128]{1,0:T(8,128)(2,1)}, bf16[128,128]{1,0:T(8,128)(2,1)S(1)}, u32[]{:S(2)}, u32[]{:S(2)}) collective-permute-start(bf16[128,128]{1,0:T(8,128)(2,1)} %refs_0_.1), channel_id=1, source_target_pairs={{0,4},{2,6},{4,8},{6,10},{8,12},{10,14},{12,0},{14,2},{1,15},{3,13... | collective-permute-start | bytes 98312 | tf_op jit(solution)/shard_map/ppermute | solution.py:156
  5.6 2.2 %collective-permute-start.3 = (bf16[128,128]{1,0:T(8,128)(2,1)}, bf16[128,128]{1,0:T(8,128)(2,1)S(1)}, u32[]{:S(2)}, u32[]{:S(2)}) collective-permute-start(bf16[128,128]{1,0:T(8,128)(2,1)} %refs_0_.1), channel_id=1, source_target_pairs={{0,12},{2,14},{4,0},{6,2},{8,4},{10,6},{12,8},{14,10},{1,11},{3,9}... | collective-permute-start | bytes 98312 | tf_op jit(solution)/shard_map/ppermute | solution.py:156
  7.9 1.5 %collective-permute-start.1 = (bf16[128,128]{1,0:T(8,128)(2,1)}, bf16[128,128]{1,0:T(8,128)(2,1)S(1)}, u32[]{:S(2)}, u32[]{:S(2)}) collective-permute-start(bf16[128,128]{1,0:T(8,128)(2,1)} %refs_0_.1), channel_id=1, source_target_pairs={{0,2},{2,0},{4,6},{6,4},{8,10},{10,8},{12,14},{14,12},{1,3},{3,1},... | collective-permute-start | bytes 98312 | tf_op jit(solution)/shard_map/ppermute | solution.py:156
  9.4 0.0 copy-done.4
  9.4 0.0 copy-start.1
  9.4 0.8 %copy-done.1 = bf16[32,4,128]{2,1,0:T(4,128)(2,1)S(1)} copy-done((bf16[32,4,128]{2,1,0:T(4,128)(2,1)S(1)}, bf16[32,4,128]{2,1,0:T(4,128)(2,1)}, u32[]{:S(2)}) %copy-start.1) | copy-done | bytes 32792
  10.1 0.0 copy-start.2
  10.1 0.8 %copy-done.2 = bf16[32,4,128]{2,1,0:T(4,128)(2,1)S(1)} copy-done((bf16[32,4,128]{2,1,0:T(4,128)(2,1)S(1)}, bf16[32,4,128]{2,1,0:T(4,128)(2,1)}, u32[]{:S(2)}) %copy-start.2) | copy-done | bytes 32792
  10.9 0.0 copy-start.3
  10.9 0.8 %shard_map.55 = (bf16[2,4,16,128]{3,2,1,0:T(8,128)(2,1)S(1)}, bf16[2,4,16,128]{3,2,1,0:T(8,128)(2,1)S(1)}) custom-call(s32[4]{0:T(128)S(1)} %bitcast.3, bf16[32,4,128]{2,1,0:T(4,128)(2,1)S(1)} %copy-done.1, bf16[32,4,128]{2,1,0:T(4,128)(2,1)S(1)} %copy-done.2), custom_call_target="tpu_custom_call" | custom-call | tf_op jit(solution)/shard_map/pallas_call | solution.py:163
  11.6 0.6 %collective-permute-start.7 = (bf16[2,4,16,128]{3,2,1,0:T(8,128)(2,1)S(1)}, bf16[2,4,16,128]{3,2,1,0:T(8,128)(2,1)S(1)}, u32[]{:S(2)}, u32[]{:S(2)}) collective-permute-start(bf16[2,4,16,128]{3,2,1,0:T(8,128)(2,1)S(1)} %get-tuple-element.8), channel_id=1, source_target_pairs={{0,2},{2,0},{1,3},{3,1},{4,6},{6,4},{5,7},{7,5},{8,10},{10,8},{9,1... | collective-permute-start | bytes 98312 | tf_op jit(solution)/shard_map/ppermute | solution.py:170
  12.2 0.0 collective-permute-done.refs_1_
  12.3 0.0 collective-permute-start.4
  12.3 0.0 collective-permute-done.2.refs_3_
  12.3 0.5 %collective-permute-start.5 = (bf16[128,128]{1,0:T(8,128)(2,1)S(1)}, bf16[128,128]{1,0:T(8,128)(2,1)S(1)}, u32[]{:S(2)}, u32[]{:S(2)}) collective-permute-start(bf16[128,128]{1,0:T(8,128)(2,1)S(1)} %collective-permute-done.2.refs_3_), channel_id=1, source_target_pairs={{0,1},{1,0},{2,3},{3,2},{4,5},{5,4},{6,7},{7,6},{8,9},{9,8},{10,11... | collective-permute-start | bytes 98312 | tf_op jit(solution)/shard_map/ppermute | solution.py:158
  12.8 0.0 collective-permute-done.3.refs_4_
  12.8 0.1 collective-permute-start.6
  12.8 0.0 copy-done
  12.8 0.1 dynamic-slice_bitcast_fusion
  12.9 0.1 copy.6.refs_10_
  13.0 2.6 %collective-permute-done.7.refs_9_ = bf16[2,4,16,128]{3,2,1,0:T(8,128)(2,1)S(1)} collective-permute-done((bf16[2,4,16,128]{3,2,1,0:T(8,128)(2,1)S(1)}, bf16[2,4,16,128]{3,2,1,0:T(8,128)(2,1)S(1)}, u32[]{:S(2)}, u32[]{:S(2)}) %collective-permute-start.7) | collective-permute-done | bytes 32800 | tf_op jit(solution)/shard_map/ppermute | solution.py:170
  15.6 0.0 collective-permute-done.1.refs_2_
  15.6 0.0 collective-permute-done.4.refs_5_
  15.6 0.0 collective-permute-done.5.refs_6_
  15.6 0.0 collective-permute-done.6.refs_7_
  15.7 0.0 copy-done.3
  15.7 2.7 %shard_map.56 = f32[16,64]{1,0:T(8,128)} custom-call(bf16[128,128]{1,0:T(8,128)(2,1)S(1)} %copy-done.3, bf16[128,128]{1,0:T(8,128)(2,1)S(1)} %collective-permute-done.refs_1_, bf16[128,128]{1,0:T(8,128)(2,1)S(1)} %collective-permute-done.1.refs_2_, bf16[128,128]{1,0:T(8,128)(2,1)S(1)} %collective-permute-done.2.refs_3_, ...), custom_call_target="tpu_custom_call" | custom-call | tf_op jit(solution)/shard_map/pallas_call | solution.py:172
Async XLA Ops:
  0.0 12.8 %copy-start = (s32[32]{0:T(128)S(1)}, s32[32]{0:T(128)}, u32[]{:S(2)}) copy-start(s32[32]{0:T(128)} %param.9) | copy-start | bytes 388
  0.0 9.4 %copy-start.4 = (s32[1,4,1]{1,2,0:T(1,128)S(1)}, s32[1,4,1]{1,2,0:T(1,128)}, u32[]{:S(2)}) copy-start(s32[1,4,1]{1,2,0:T(1,128)} %param.8) | copy-start | bytes 52
  0.0 12.2 %collective-permute-start = (bf16[128,128]{1,0:T(8,128)(2,1)}, bf16[128,128]{1,0:T(8,128)(2,1)S(1)}, u32[]{:S(2)}, u32[]{:S(2)}) collective-permute-start(bf16[128,128]{1,0:T(8,128)(2,1)} %refs_0_.1), channel_id=1, source_target_pairs={{0,8},{2,10},{4,12},{6,14},{8,0},{10,2},{12,4},{14,6},{1,7},{3,5},... | collective-permute-start | bytes 98312 | tf_op jit(solution)/shard_map/ppermute | solution.py:156
  4.0 8.2 %collective-permute-start.2 = (bf16[128,128]{1,0:T(8,128)(2,1)}, bf16[128,128]{1,0:T(8,128)(2,1)S(1)}, u32[]{:S(2)}, u32[]{:S(2)}) collective-permute-start(bf16[128,128]{1,0:T(8,128)(2,1)} %refs_0_.1), channel_id=1, source_target_pairs={{0,4},{2,6},{4,8},{6,10},{8,12},{10,14},{12,0},{14,2},{1,15},{3,13... | collective-permute-start | bytes 98312 | tf_op jit(solution)/shard_map/ppermute | solution.py:156
  5.6 7.2 %collective-permute-start.3 = (bf16[128,128]{1,0:T(8,128)(2,1)}, bf16[128,128]{1,0:T(8,128)(2,1)S(1)}, u32[]{:S(2)}, u32[]{:S(2)}) collective-permute-start(bf16[128,128]{1,0:T(8,128)(2,1)} %refs_0_.1), channel_id=1, source_target_pairs={{0,12},{2,14},{4,0},{6,2},{8,4},{10,6},{12,8},{14,10},{1,11},{3,9}... | collective-permute-start | bytes 98312 | tf_op jit(solution)/shard_map/ppermute | solution.py:156
  7.9 7.8 %collective-permute-start.1 = (bf16[128,128]{1,0:T(8,128)(2,1)}, bf16[128,128]{1,0:T(8,128)(2,1)S(1)}, u32[]{:S(2)}, u32[]{:S(2)}) collective-permute-start(bf16[128,128]{1,0:T(8,128)(2,1)} %refs_0_.1), channel_id=1, source_target_pairs={{0,2},{2,0},{4,6},{6,4},{8,10},{10,8},{12,14},{14,12},{1,3},{3,1},... | collective-permute-start | bytes 98312 | tf_op jit(solution)/shard_map/ppermute | solution.py:156
  9.4 0.8 %copy-start.1 = (bf16[32,4,128]{2,1,0:T(4,128)(2,1)S(1)}, bf16[32,4,128]{2,1,0:T(4,128)(2,1)}, u32[]{:S(2)}) copy-start(bf16[32,4,128]{2,1,0:T(4,128)(2,1)} %confidence_ref.1) | copy-start | bytes 98308
  10.1 0.8 %copy-start.2 = (bf16[32,4,128]{2,1,0:T(4,128)(2,1)S(1)}, bf16[32,4,128]{2,1,0:T(4,128)(2,1)}, u32[]{:S(2)}) copy-start(bf16[32,4,128]{2,1,0:T(4,128)(2,1)} %ratings_ref.1) | copy-start | bytes 98308
  10.9 4.8 %copy-start.3 = (bf16[128,128]{1,0:T(8,128)(2,1)S(1)}, bf16[128,128]{1,0:T(8,128)(2,1)}, u32[]{:S(2)}) copy-start(bf16[128,128]{1,0:T(8,128)(2,1)} %refs_0_.1) | copy-start | bytes 98308
  11.6 4.0 %collective-permute-start.7 = (bf16[2,4,16,128]{3,2,1,0:T(8,128)(2,1)S(1)}, bf16[2,4,16,128]{3,2,1,0:T(8,128)(2,1)S(1)}, u32[]{:S(2)}, u32[]{:S(2)}) collective-permute-start(bf16[2,4,16,128]{3,2,1,0:T(8,128)(2,1)S(1)} %get-tuple-element.8), channel_id=1, source_target_pairs={{0,2},{2,0},{1,3},{3,1},{4,6},{6,4},{5,7},{7,5},{8,10},{10,8},{9,1... | collective-permute-start | bytes 98312 | tf_op jit(solution)/shard_map/ppermute | solution.py:170
  12.3 3.4 %collective-permute-start.4 = (bf16[128,128]{1,0:T(8,128)(2,1)S(1)}, bf16[128,128]{1,0:T(8,128)(2,1)S(1)}, u32[]{:S(2)}, u32[]{:S(2)}) collective-permute-start(bf16[128,128]{1,0:T(8,128)(2,1)S(1)} %collective-permute-done.refs_1_), channel_id=1, source_target_pairs={{0,1},{1,0},{2,3},{3,2},{4,5},{5,4},{6,7},{7,6},{8,9},{9,8},{10,11... | collective-permute-start | bytes 98312 | tf_op jit(solution)/shard_map/ppermute | solution.py:158
  12.3 3.4 %collective-permute-start.5 = (bf16[128,128]{1,0:T(8,128)(2,1)S(1)}, bf16[128,128]{1,0:T(8,128)(2,1)S(1)}, u32[]{:S(2)}, u32[]{:S(2)}) collective-permute-start(bf16[128,128]{1,0:T(8,128)(2,1)S(1)} %collective-permute-done.2.refs_3_), channel_id=1, source_target_pairs={{0,1},{1,0},{2,3},{3,2},{4,5},{5,4},{6,7},{7,6},{8,9},{9,8},{10,11... | collective-permute-start | bytes 98312 | tf_op jit(solution)/shard_map/ppermute | solution.py:158
  12.8 2.9 %collective-permute-start.6 = (bf16[128,128]{1,0:T(8,128)(2,1)S(1)}, bf16[128,128]{1,0:T(8,128)(2,1)S(1)}, u32[]{:S(2)}, u32[]{:S(2)}) collective-permute-start(bf16[128,128]{1,0:T(8,128)(2,1)S(1)} %collective-permute-done.3.refs_4_), channel_id=1, source_target_pairs={{0,1},{1,0},{2,3},{3,2},{4,5},{5,4},{6,7},{7,6},{8,9},{9,8},{10,11... | collective-permute-start | bytes 98312 | tf_op jit(solution)/shard_map/ppermute | solution.py:158

commit v3 on v2

--- a/solution.py
+++ b/solution.py
@@ -15,11 +15,9 @@
 
 PLACE = ("blk", "grp", "rep")
 LINE = (0, 1, 2, 3)
-FOLDED = (0, 1, 3, 2)
 EXCHANGES = (
-    ((LINE, 2, 0), (LINE, 1, 1)),
-    ((LINE, 0, 1), (LINE, 0, 1)),
-    ((LINE, 1, 0), (LINE, 3, 1)),
+    ((LINE, 1, 0), (LINE, 2, 0)),
+    ((LINE, 1, 1), (LINE, 3, 1)),
     ((LINE, 3, 0), (LINE, 2, 1)),
 )
 
@@ -58,15 +56,18 @@
     return value[:rows] + value[rows:]
 
 
+def row_sums(value):
+    return jnp.sum(value, axis=1, keepdims=True)
+
+
 def conjugate_gradient(factors, weighted, paired, ridge):
     rows = weighted.shape[0]
     weights = weighted + unobserved_weight
-    right_side = jnp.dot(paired, factors, preferred_element_type=jnp.float32)
-
-    def project(direction):
+
+    def project(vector):
         return joined(
             lax.dot_general(
-                halves(direction),
+                halves(vector),
                 factors,
                 (((1,), (1,)), ((), ())),
                 preferred_element_type=jnp.float32,
@@ -80,19 +81,23 @@
             rows,
         )
 
-    total = jnp.zeros_like(right_side)
-    residual = right_side
-    direction = right_side
-    norm_now = jnp.sum(residual * residual, axis=1, keepdims=True)
+    residual = jnp.dot(paired, factors, preferred_element_type=jnp.float32)
+    direction = residual
+    projected = project(residual)
+    norm_now = row_sums(residual * residual)
+    total = jnp.zeros_like(residual)
     for turn in range(CG_STEPS):
-        image = back(project(direction) * weights) + ridge * direction
-        step_size = norm_now / (jnp.sum(direction * image, axis=1, keepdims=True) + epsilon)
+        weighed = weights * projected
+        curvature = row_sums(weighed * projected) + ridge * row_sums(direction * direction)
+        step_size = norm_now / (curvature + epsilon)
         total = total + step_size * direction
         if turn == CG_STEPS - 1:
             break
-        residual = residual - step_size * image
-        norm_next = jnp.sum(residual * residual, axis=1, keepdims=True)
-        direction = residual + (norm_next / (norm_now + epsilon)) * direction
+        residual = residual - step_size * (back(weighed) + ridge * direction)
+        norm_next = row_sums(residual * residual)
+        ratio = norm_next / (norm_now + epsilon)
+        projected = project(residual) + ratio * projected
+        direction = residual + ratio * direction
         norm_now = norm_next
     return total
 
@@ -104,79 +109,134 @@
     return chosen
 
 
-def pair_kernel(flags_ref, confidence_ref, ratings_ref, mine_ref, theirs_ref):
+def packet_kernel(
+    flags_ref,
+    confidence_ref,
+    ratings_ref,
+    factors_ref,
+    counts_ref,
+    earlier_ref,
+    mine_ref,
+    theirs_ref,
+    ridge_ref,
+    weight_ref,
+    rating_ref,
+    count_ref,
+    value_ref,
+    arrived,
+):
+    del earlier_ref
     group = lax.axis_index("grp")
     users, cycle_size, tile_items = confidence_ref.shape
     owned = users // 2
-    weight = confidence_ref[...].astype(jnp.float32)
-    rating = ratings_ref[...].astype(jnp.float32)
-    for source in range(cycle_size):
-        flag = flags_ref[source] != 0
-        masked = jnp.where(flag, weight[:, source, :], 0.0)
-        product = masked * rating[:, source, :]
-        for kind, value in enumerate((masked, product)):
-            value = value.astype(jnp.bfloat16)
-            first, second = value[:owned], value[owned:]
-            mine_ref[kind, source] = jnp.where(group == 0, first, second)
-            theirs_ref[kind, source] = jnp.where(group == 0, second, first)
+    copies = [
+        pltpu.make_async_copy(source, target, arrived.at[number])
+        for number, (source, target) in enumerate(
+            (
+                (confidence_ref, weight_ref),
+                (ratings_ref, rating_ref),
+                (factors_ref, mine_ref.at[pl.ds(0, tile_items)]),
+                (factors_ref, theirs_ref.at[pl.ds(0, tile_items)]),
+                (counts_ref, count_ref),
+            )
+        )
+    ]
+    for copy in copies:
+        copy.start()
+    copies[0].wait()
+    copies[1].wait()
+    rows = users * cycle_size
+    weight = weight_ref[...].astype(jnp.float32).reshape(rows, tile_items)
+    rating = rating_ref[...].astype(jnp.float32).reshape(rows, tile_items)
+    source = lax.rem(lax.broadcasted_iota(jnp.int32, (rows, tile_items), 0), cycle_size)
+    flag = jnp.zeros_like(source)
+    for number in range(cycle_size):
+        flag = jnp.where(source == number, flags_ref[number], flag)
+    weight = jnp.where(flag != 0, weight, 0.0)
+    for kind, value in enumerate((weight, weight * rating)):
+        value_ref[kind] = value
+        for number in range(cycle_size):
+            target = pl.ds(tile_items + (kind * cycle_size + number) * owned, owned)
+            for packet_ref, half in ((mine_ref, group), (theirs_ref, 1 - group)):
+                start = half * (owned * cycle_size) + number
+                packet_ref[target] = value_ref[
+                    kind, pl.ds(start, owned, stride=cycle_size)
+                ].astype(jnp.bfloat16)
+    for copy in copies[2:]:
+        copy.wait()
+    user = lax.broadcasted_iota(jnp.int32, (owned, users), 0) + group * owned
+    entry = lax.broadcasted_iota(jnp.int32, user.shape, 1)
+    counts = row_sums(jnp.where(user == entry, count_ref[...].astype(jnp.float32), 0.0))
+    ridge_ref[...] = jnp.broadcast_to(regular_weight * counts, ridge_ref.shape)
 
 
 def chip_kernel(*refs):
-    own_ref, *block_refs, mine_ref, theirs_ref, counts_ref, out_ref, held = refs
+    *block_refs, mine_ref, theirs_ref, ridge_ref, out_ref, held = refs
     position = lax.axis_index("blk")
     core = lax.axis_index("rep")
-    cycle_size, dim = mine_ref.shape[1], own_ref.shape[1]
-    held[position] = own_ref[...]
-    direct = block_refs[: len(EXCHANGES)]
-    passed = list(block_refs[len(EXCHANGES) :])
-    for rules, block_ref in zip(EXCHANGES, direct):
-        slots = [source_slot(rule, position) for rule in rules]
-        held[jnp.where(core == 0, slots[0], slots[1])] = block_ref[...]
-        if rules[0] != rules[1]:
-            held[jnp.where(core == 0, slots[1], slots[0])] = passed.pop(0)[...]
+    slots, tile_items, dim = held.shape
+    owned, cycle_size = out_ref.shape[0], slots // 2
+    for number, rules in enumerate(EXCHANGES):
+        places = [source_slot(rule, position) for rule in rules]
+        direct, passed = block_refs[number], block_refs[len(EXCHANGES) + number]
+        held[jnp.where(core == 0, places[0], places[1])] = direct[...]
+        held[jnp.where(core == 0, places[1], places[0])] = passed[...]
+    held[position] = mine_ref[:tile_items]
+    held[cycle_size + position] = theirs_ref[:tile_items]
     factors = held[...].reshape(-1, dim)
-    blocks = [ref.at[:, source] for ref in (mine_ref, theirs_ref) for source in range(cycle_size)]
-    weighted = jnp.concatenate([block[0] for block in blocks], axis=1).astype(jnp.float32)
-    paired = jnp.concatenate([block[1] for block in blocks], axis=1)
-    ridge = regular_weight * counts_ref[...].astype(jnp.float32)
-    total = conjugate_gradient(factors, weighted, paired, ridge)
+
+    def joined_tiles(kind):
+        rows = [
+            pl.ds(tile_items + (kind * cycle_size + source) * owned, owned)
+            for source in range(cycle_size)
+        ]
+        return jnp.concatenate([ref[row] for ref in (mine_ref, theirs_ref) for row in rows], axis=1)
+
+    weighted = joined_tiles(0).astype(jnp.float32)
+    total = conjugate_gradient(factors, weighted, joined_tiles(1), ridge_ref[...])
     out_ref[...] = columns_of(total, core, out_ref.shape[1])
 
 
 VMEM = pl.BlockSpec(memory_space=pltpu.VMEM)
 SMEM = pl.BlockSpec(memory_space=pltpu.SMEM)
+HBM = pl.BlockSpec(memory_space=pltpu.HBM)
 
 
 def chip_shards(item_factors, confidence, ratings, pattern, counts):
     tile_items, dim = item_factors.shape
     users, cycle_size = confidence.shape[:2]
     owned = users // 2
-    group = lax.axis_index("grp")
     swap = [(0, 1), (1, 0)]
     direct = [lax.ppermute(item_factors, PLACE, exchange_route(rules)) for rules in EXCHANGES]
-    passed = [
-        lax.ppermute(block, "rep", swap)
-        for rules, block in zip(EXCHANGES, direct)
-        if rules[0] != rules[1]
-    ]
-    half_shape = jax.ShapeDtypeStruct((2, cycle_size, owned, tile_items), jnp.bfloat16)
-    mine, theirs = pl.pallas_call(
-        pair_kernel,
-        out_shape=(half_shape, half_shape),
-        in_specs=[SMEM, VMEM, VMEM],
-        out_specs=(VMEM, VMEM),
+    passed = [lax.ppermute(block, "rep", swap) for block in direct]
+    packet_inputs = (pattern[0, :, 0], confidence, ratings, item_factors, counts[None])
+    packet = jax.ShapeDtypeStruct((tile_items + 2 * cycle_size * owned, dim), jnp.bfloat16)
+    ridge = jax.ShapeDtypeStruct((owned, dim), jnp.float32)
+    mine, theirs, ridge = pl.pallas_call(
+        packet_kernel,
+        out_shape=(packet, packet, ridge),
+        in_specs=[SMEM, HBM, HBM, HBM, HBM, VMEM],
+        out_specs=(VMEM, VMEM, VMEM),
+        scratch_shapes=[
+            pltpu.VMEM(confidence.shape, jnp.bfloat16),
+            pltpu.VMEM(ratings.shape, jnp.bfloat16),
+            pltpu.VMEM((1, users), jnp.int32),
+            pltpu.VMEM((2, users * cycle_size, tile_items), jnp.float32),
+            pltpu.SemaphoreType.DMA((5,)),
+        ],
         compiler_params=pltpu.CompilerParams(vmem_limit_bytes=8 * 1024 * 1024),
-    )(pattern[0, :, 0], confidence, ratings)
+    )(
+        *(pltpu.with_memory_space_constraint(array, pltpu.HBM) for array in packet_inputs), direct[0]
+    )
     theirs = lax.ppermute(theirs, "grp", swap)
-    owned_counts = lax.dynamic_slice_in_dim(counts, group * owned, owned, 0)[:, None]
     return pl.pallas_call(
         chip_kernel,
         out_shape=jax.ShapeDtypeStruct((owned, dim // 2), jnp.float32),
-        in_specs=[VMEM] * (4 + len(direct) + len(passed)),
+        in_specs=[VMEM] * (3 + len(direct) + len(passed)),
         out_specs=VMEM,
         scratch_shapes=[pltpu.VMEM((2 * cycle_size, tile_items, dim), jnp.bfloat16)],
         compiler_params=pltpu.CompilerParams(vmem_limit_bytes=8 * 1024 * 1024),
-    )(item_factors, *direct, *passed, mine, theirs, owned_counts)
+    )(*direct, *passed, mine, theirs, ridge)
 
 
 def gathered_kernel(factors_ref, pair_ref, counts_ref, out_ref):

time: 18.6 us -> 16 us (0.86)
  local copies, waits for them, and re-layouts: 1.69 us -> 0 us
  starting transfers between devices: 10.5 us -> 9.5 us
  Pallas kernels: 3.44 us -> 3.69 us
    ppermute x4 -> x3, starting transfers between devices: 9.35 us -> 7.77 us  [chip_shards(): lax.ppermute(item_factors, PLACE, exchange_route(rules))]
    unnamed x10 -> x0, local copies, waits for them, and re-layouts: 1.53 us -> none
    ppermute x1, waiting for transfers between devices: 2.62 us -> 1.46 us  [chip_shards(): theirs = lax.ppermute(theirs, 'grp', swap)]
    ppermute x3, waiting for transfers between devices: 0.01 us -> 1.14 us  [chip_shards(): passed = [lax.ppermute(block, 'rep', swap) for block in direct]]
    pallas_call x1, Pallas kernels: 0.76 us -> 1.64 us  [chip_shards(): pl.pallas_call(packet_kernel, out_shape=(packet, packet, ridge), in_specs...]
    pallas_call x1, Pallas kernels: 2.67 us -> 2.05 us  [chip_shards(): pl.pallas_call(chip_kernel, out_shape=jax.ShapeDtypeStruct((owned, dim //...]
    ppermute x1, starting transfers between devices: 0.6 us -> 1.15 us  [chip_shards(): theirs = lax.ppermute(theirs, 'grp', swap)]
  transfers between devices with their start and end apart: 8 -> 7, of which waited for: 1 -> 4; matrix products, arithmetic and copies ran while one was open for 1% -> 0% of each run, Pallas kernels for 4% -> 10%
where the time goes in v3:
time: 16 us; the launch traced here: 15.8 us
  starting transfers between devices  9.5 us (59%)
  Pallas kernels  3.69 us (23%)
  waiting for transfers between devices  2.6 us (16%)
    ppermute x3, starting transfers between devices, chip_shards(): lax.ppermute(item_factors, PLACE, exchange_route(rules))  7.77 us
    pallas_call x1, Pallas kernels, chip_shards(): pl.pallas_call(chip_kernel, out_shape=jax.ShapeDtypeStruct((owned, dim //...  2.05 us
    pallas_call x1, Pallas kernels, chip_shards(): pl.pallas_call(packet_kernel, out_shape=(packet, packet, ridge), in_specs...  1.64 us
    ppermute x1, waiting for transfers between devices, chip_shards(): theirs = lax.ppermute(theirs, 'grp', swap)  1.46 us
    ppermute x1, starting transfers between devices, chip_shards(): theirs = lax.ppermute(theirs, 'grp', swap)  1.15 us
    ppermute x3, waiting for transfers between devices, chip_shards(): passed = [lax.ppermute(block, 'rep', swap) for block in direct]  1.14 us
    ppermute x3, starting transfers between devices, chip_shards(): passed = [lax.ppermute(block, 'rep', swap) for block in direct]  0.58 us
  transfers between devices with their start and end apart: 7, of which 4 were waited for; matrix products, arithmetic and copies ran while one was open for 0% of the time, Pallas kernels for 10%

profile of v3, /device:TPU:0, one launch (start us, length us, event | category | flops | bytes accessed | tf_op | source)
XLA Modules:
  0.0 15.8 jit_solution(15629204091517087)
XLA Ops:
  0.0 3.0 %collective-permute-start = (bf16[128,128]{1,0:T(8,128)(2,1)}, bf16[128,128]{1,0:T(8,128)(2,1)S(1)}, u32[]{:S(2)}, u32[]{:S(2)}) collective-permute-start(bf16[128,128]{1,0:T(8,128)(2,1)} %factors_ref.1), channel_id=1, source_target_pairs={{0,4},{2,6},{4,8},{6,10},{8,12},{10,14},{12,0},{14,2},{1,9},{3,11}... | collective-permute-start | bytes 98312 | tf_op jit(solution)/shard_map/ppermute | solution.py:210
  3.0 2.5 %collective-permute-start.1 = (bf16[128,128]{1,0:T(8,128)(2,1)}, bf16[128,128]{1,0:T(8,128)(2,1)S(1)}, u32[]{:S(2)}, u32[]{:S(2)}) collective-permute-start(bf16[128,128]{1,0:T(8,128)(2,1)} %factors_ref.1), channel_id=1, source_target_pairs={{0,6},{2,4},{4,10},{6,8},{8,14},{10,12},{12,2},{14,0},{1,15},{3,13... | collective-permute-start | bytes 98312 | tf_op jit(solution)/shard_map/ppermute | solution.py:210
  5.5 2.2 %collective-permute-start.2 = (bf16[128,128]{1,0:T(8,128)(2,1)}, bf16[128,128]{1,0:T(8,128)(2,1)S(1)}, u32[]{:S(2)}, u32[]{:S(2)}) collective-permute-start(bf16[128,128]{1,0:T(8,128)(2,1)} %factors_ref.1), channel_id=1, source_target_pairs={{0,12},{2,14},{4,0},{6,2},{8,4},{10,6},{12,8},{14,10},{1,11},{3,9}... | collective-permute-start | bytes 98312 | tf_op jit(solution)/shard_map/ppermute | solution.py:210
  7.8 0.0 collective-permute-done.earlier_ref.refs_0_
  7.8 1.6 %shard_map.55 = (bf16[256,128]{1,0:T(8,128)(2,1)S(1)}, bf16[256,128]{1,0:T(8,128)(2,1)S(1)}, f32[16,128]{1,0:T(8,128)S(1)}) custom-call(s32[4]{0:T(128)} %bitcast.2, bf16[32,4,128]{2,1,0:T(4,128)(2,1)} %confidence_ref.1, bf16[32,4,128]{2,1,0:T(4,128)(2,1)} %ratings_ref.1, bf16[128,128]{1,0:T(8,128)(2,1)} %factors_ref.1, s32[1,32]{1,0:T(1,128)} %bitcast.3, ...), custom_call_target="tpu_custom_call" | custom-call | tf_op jit(solution)/shard_map/pallas_call | solution.py:215
  9.4 1.1 %collective-permute-start.6 = (bf16[256,128]{1,0:T(8,128)(2,1)S(1)}, bf16[256,128]{1,0:T(8,128)(2,1)S(1)}, u32[]{:S(2)}, u32[]{:S(2)}) collective-permute-start(bf16[256,128]{1,0:T(8,128)(2,1)S(1)} %get-tuple-element.9), channel_id=1, source_target_pairs={{0,2},{2,0},{1,3},{3,1},{4,6},{6,4},{5,7},{7,5},{8,10},{10,8},{9,1... | collective-permute-start | bytes 196616 | tf_op jit(solution)/shard_map/ppermute | solution.py:231
  10.6 0.0 collective-permute-start.3
  10.6 0.0 collective-permute-done.1.refs_1_
  10.6 0.5 %collective-permute-start.4 = (bf16[128,128]{1,0:T(8,128)(2,1)S(1)}, bf16[128,128]{1,0:T(8,128)(2,1)S(1)}, u32[]{:S(2)}, u32[]{:S(2)}) collective-permute-start(bf16[128,128]{1,0:T(8,128)(2,1)S(1)} %collective-permute-done.1.refs_1_), channel_id=1, source_target_pairs={{0,1},{1,0},{2,3},{3,2},{4,5},{5,4},{6,7},{7,6},{8,9},{9,8},{10,11... | collective-permute-start | bytes 98312 | tf_op jit(solution)/shard_map/ppermute | solution.py:211
  11.1 0.0 collective-permute-done.2.refs_2_
  11.1 0.1 collective-permute-start.5
  11.2 0.6 %collective-permute-done.3.refs_3_ = bf16[128,128]{1,0:T(8,128)(2,1)S(1)} collective-permute-done((bf16[128,128]{1,0:T(8,128)(2,1)S(1)}, bf16[128,128]{1,0:T(8,128)(2,1)S(1)}, u32[]{:S(2)}, u32[]{:S(2)}) %collective-permute-start.3) | collective-permute-done | bytes 32800 | tf_op jit(solution)/shard_map/ppermute | solution.py:211
  11.8 0.2 %collective-permute-done.4.refs_4_ = bf16[128,128]{1,0:T(8,128)(2,1)S(1)} collective-permute-done((bf16[128,128]{1,0:T(8,128)(2,1)S(1)}, bf16[128,128]{1,0:T(8,128)(2,1)S(1)}, u32[]{:S(2)}, u32[]{:S(2)}) %collective-permute-start.4) | collective-permute-done | bytes 32800 | tf_op jit(solution)/shard_map/ppermute | solution.py:211
  11.9 0.4 %collective-permute-done.5.refs_5_ = bf16[128,128]{1,0:T(8,128)(2,1)S(1)} collective-permute-done((bf16[128,128]{1,0:T(8,128)(2,1)S(1)}, bf16[128,128]{1,0:T(8,128)(2,1)S(1)}, u32[]{:S(2)}, u32[]{:S(2)}) %collective-permute-start.5) | collective-permute-done | bytes 32800 | tf_op jit(solution)/shard_map/ppermute | solution.py:211
  12.3 1.5 %collective-permute-done.6.refs_7_ = bf16[256,128]{1,0:T(8,128)(2,1)S(1)} collective-permute-done((bf16[256,128]{1,0:T(8,128)(2,1)S(1)}, bf16[256,128]{1,0:T(8,128)(2,1)S(1)}, u32[]{:S(2)}, u32[]{:S(2)}) %collective-permute-start.6) | collective-permute-done | bytes 65568 | tf_op jit(solution)/shard_map/ppermute | solution.py:231
  13.8 2.1 %shard_map.56 = f32[16,64]{1,0:T(8,128)} custom-call(bf16[128,128]{1,0:T(8,128)(2,1)S(1)} %collective-permute-done.earlier_ref.refs_0_, bf16[128,128]{1,0:T(8,128)(2,1)S(1)} %collective-permute-done.1.refs_1_, bf16[128,128]{1,0:T(8,128)(2,1)S(1)} %collective-permute-done.2.refs_2_, bf16[128,128]{1,0:T(8,128)(2,1)S(1)} %collective-permute-done.3.refs_3_, ...), custom_call_target="tpu_custom_call" | custom-call | tf_op jit(solution)/shard_map/pallas_call | solution.py:232
Async XLA Ops:
  0.0 7.8 %collective-permute-start = (bf16[128,128]{1,0:T(8,128)(2,1)}, bf16[128,128]{1,0:T(8,128)(2,1)S(1)}, u32[]{:S(2)}, u32[]{:S(2)}) collective-permute-start(bf16[128,128]{1,0:T(8,128)(2,1)} %factors_ref.1), channel_id=1, source_target_pairs={{0,4},{2,6},{4,8},{6,10},{8,12},{10,14},{12,0},{14,2},{1,9},{3,11}... | collective-permute-start | bytes 98312 | tf_op jit(solution)/shard_map/ppermute | solution.py:210
  3.0 7.6 %collective-permute-start.1 = (bf16[128,128]{1,0:T(8,128)(2,1)}, bf16[128,128]{1,0:T(8,128)(2,1)S(1)}, u32[]{:S(2)}, u32[]{:S(2)}) collective-permute-start(bf16[128,128]{1,0:T(8,128)(2,1)} %factors_ref.1), channel_id=1, source_target_pairs={{0,6},{2,4},{4,10},{6,8},{8,14},{10,12},{12,2},{14,0},{1,15},{3,13... | collective-permute-start | bytes 98312 | tf_op jit(solution)/shard_map/ppermute | solution.py:210
  5.5 5.6 %collective-permute-start.2 = (bf16[128,128]{1,0:T(8,128)(2,1)}, bf16[128,128]{1,0:T(8,128)(2,1)S(1)}, u32[]{:S(2)}, u32[]{:S(2)}) collective-permute-start(bf16[128,128]{1,0:T(8,128)(2,1)} %factors_ref.1), channel_id=1, source_target_pairs={{0,12},{2,14},{4,0},{6,2},{8,4},{10,6},{12,8},{14,10},{1,11},{3,9}... | collective-permute-start | bytes 98312 | tf_op jit(solution)/shard_map/ppermute | solution.py:210
  9.4 4.3 %collective-permute-start.6 = (bf16[256,128]{1,0:T(8,128)(2,1)S(1)}, bf16[256,128]{1,0:T(8,128)(2,1)S(1)}, u32[]{:S(2)}, u32[]{:S(2)}) collective-permute-start(bf16[256,128]{1,0:T(8,128)(2,1)S(1)} %get-tuple-element.9), channel_id=1, source_target_pairs={{0,2},{2,0},{1,3},{3,1},{4,6},{6,4},{5,7},{7,5},{8,10},{10,8},{9,1... | collective-permute-start | bytes 196616 | tf_op jit(solution)/shard_map/ppermute | solution.py:231
  10.6 1.2 %collective-permute-start.3 = (bf16[128,128]{1,0:T(8,128)(2,1)S(1)}, bf16[128,128]{1,0:T(8,128)(2,1)S(1)}, u32[]{:S(2)}, u32[]{:S(2)}) collective-permute-start(bf16[128,128]{1,0:T(8,128)(2,1)S(1)} %collective-permute-done.earlier_ref.refs_0_), channel_id=1, source_target_pairs={{0,1},{1,0},{2,3},{3,2},{4,5},{5,4},{6,7},{7,6},{8,9},{9,8},{10,11... | collective-permute-start | bytes 98312 | tf_op jit(solution)/shard_map/ppermute | solution.py:211
  10.6 1.4 %collective-permute-start.4 = (bf16[128,128]{1,0:T(8,128)(2,1)S(1)}, bf16[128,128]{1,0:T(8,128)(2,1)S(1)}, u32[]{:S(2)}, u32[]{:S(2)}) collective-permute-start(bf16[128,128]{1,0:T(8,128)(2,1)S(1)} %collective-permute-done.1.refs_1_), channel_id=1, source_target_pairs={{0,1},{1,0},{2,3},{3,2},{4,5},{5,4},{6,7},{7,6},{8,9},{9,8},{10,11... | collective-permute-start | bytes 98312 | tf_op jit(solution)/shard_map/ppermute | solution.py:211
  11.1 1.2 %collective-permute-start.5 = (bf16[128,128]{1,0:T(8,128)(2,1)S(1)}, bf16[128,128]{1,0:T(8,128)(2,1)S(1)}, u32[]{:S(2)}, u32[]{:S(2)}) collective-permute-start(bf16[128,128]{1,0:T(8,128)(2,1)S(1)} %collective-permute-done.2.refs_2_), channel_id=1, source_target_pairs={{0,1},{1,0},{2,3},{3,2},{4,5},{5,4},{6,7},{7,6},{8,9},{9,8},{10,11... | collective-permute-start | bytes 98312 | tf_op jit(solution)/shard_map/ppermute | solution.py:211

commit v4 on v3

--- a/solution.py
+++ b/solution.py
@@ -14,24 +14,24 @@
 epsilon = 1e-06
 
 PLACE = ("blk", "grp", "rep")
-LINE = (0, 1, 2, 3)
+ADD, FLIP = "add", "flip"
 EXCHANGES = (
-    ((LINE, 1, 0), (LINE, 2, 0)),
-    ((LINE, 1, 1), (LINE, 3, 1)),
-    ((LINE, 3, 0), (LINE, 2, 1)),
+    ((FLIP, 1, 1), (ADD, 1, 0)),
+    ((FLIP, 2, 1), (FLIP, 3, 1)),
+    ((ADD, 3, 0), (ADD, 2, 0)),
 )
 
 
-def stepped(order, position, steps):
-    return order[(order.index(position) + steps) % len(order)]
+def stepped(change, position, steps):
+    return position ^ abs(steps) if change == FLIP else (position + steps) % 4
 
 
 def exchange_route(rules):
     route = []
-    for core, (order, steps, other) in enumerate(rules):
+    for core, (change, steps, other) in enumerate(rules):
         for position in range(4):
             for group in range(2):
-                target = stepped(order, position, steps)
+                target = stepped(change, position, steps)
                 route.append(
                     ((position * 2 + group) * 2 + core, (target * 2 + (group ^ other)) * 2 + core)
                 )
@@ -39,11 +39,12 @@
 
 
 def source_slot(rule, position):
-    order, steps, other = rule
-    slot = jnp.int32(0)
-    for target in range(4):
-        slot = jnp.where(position == target, 4 * other + stepped(order, target, -steps), slot)
-    return slot
+    change, steps, other = rule
+    if change == FLIP:
+        source = lax.bitwise_xor(position, steps)
+    else:
+        source = lax.bitwise_and(position - steps, 3)
+    return 4 * other + source
 
 
 def halves(value):

time: 16 us -> 14.7 us (0.919)
  starting transfers between devices: 9.5 us -> 8.8 us
  waiting for transfers between devices: 2.6 us -> 2.04 us
    ppermute x3, starting transfers between devices: 7.77 us -> 6.51 us  [chip_shards(): lax.ppermute(item_factors, PLACE, exchange_route(rules))]
    ppermute x1, waiting for transfers between devices: 1.46 us -> 0.49 us  [chip_shards(): theirs = lax.ppermute(theirs, 'grp', swap)]
    ppermute x3, waiting for transfers between devices: 0.01 us -> 0.69 us  [chip_shards(): lax.ppermute(item_factors, PLACE, exchange_route(rules))]
    ppermute x1, starting transfers between devices: 1.15 us -> 1.77 us  [chip_shards(): theirs = lax.ppermute(theirs, 'grp', swap)]
    ppermute x3, waiting for transfers between devices: 1.14 us -> 0.86 us  [chip_shards(): passed = [lax.ppermute(block, 'rep', swap) for block in direct]]
  transfers between devices with their start and end apart: 7 -> 7, of which waited for: 4 -> 4; matrix products, arithmetic and copies ran while one was open for 0% -> 0% of each run, Pallas kernels for 10% -> 11%
where the time goes in v4:
time: 14.7 us; the launch traced here: 14.6 us
  starting transfers between devices  8.8 us (60%)
  Pallas kernels  3.69 us (25%)
  waiting for transfers between devices  2.04 us (14%)
    ppermute x3, starting transfers between devices, chip_shards(): lax.ppermute(item_factors, PLACE, exchange_route(rules))  6.51 us
    pallas_call x1, Pallas kernels, chip_shards(): pl.pallas_call(chip_kernel, out_shape=jax.ShapeDtypeStruct((owned, dim //...  2.06 us
    ppermute x1, starting transfers between devices, chip_shards(): theirs = lax.ppermute(theirs, 'grp', swap)  1.77 us
    pallas_call x1, Pallas kernels, chip_shards(): pl.pallas_call(packet_kernel, out_shape=(packet, packet, ridge), in_specs...  1.64 us
    ppermute x3, waiting for transfers between devices, chip_shards(): passed = [lax.ppermute(block, 'rep', swap) for block in direct]  0.86 us
    ppermute x3, waiting for transfers between devices, chip_shards(): lax.ppermute(item_factors, PLACE, exchange_route(rules))  0.69 us
    ppermute x3, starting transfers between devices, chip_shards(): passed = [lax.ppermute(block, 'rep', swap) for block in direct]  0.51 us
    ppermute x1, waiting for transfers between devices, chip_shards(): theirs = lax.ppermute(theirs, 'grp', swap)  0.49 us
  transfers between devices with their start and end apart: 7, of which 4 were waited for; matrix products, arithmetic and copies ran while one was open for 0% of the time, Pallas kernels for 11%

profile of v4, /device:TPU:0, one launch (start us, length us, event | category | flops | bytes accessed | tf_op | source)
XLA Modules:
  0.0 14.6 jit_solution(16679901731081643067)
XLA Ops:
  0.0 4.0 %collective-permute-start = (bf16[128,128]{1,0:T(8,128)(2,1)}, bf16[128,128]{1,0:T(8,128)(2,1)S(1)}, u32[]{:S(2)}, u32[]{:S(2)}) collective-permute-start(bf16[128,128]{1,0:T(8,128)(2,1)} %factors_ref.1), channel_id=1, source_target_pairs={{0,6},{2,4},{4,2},{6,0},{8,14},{10,12},{12,10},{14,8},{1,5},{3,7},... | collective-permute-start | bytes 98312 | tf_op jit(solution)/shard_map/ppermute | solution.py:211
  4.0 2.6 %collective-permute-start.1 = (bf16[128,128]{1,0:T(8,128)(2,1)}, bf16[128,128]{1,0:T(8,128)(2,1)S(1)}, u32[]{:S(2)}, u32[]{:S(2)}) collective-permute-start(bf16[128,128]{1,0:T(8,128)(2,1)} %factors_ref.1), channel_id=1, source_target_pairs={{0,10},{2,8},{4,14},{6,12},{8,2},{10,0},{12,6},{14,4},{1,15},{3,13... | collective-permute-start | bytes 98312 | tf_op jit(solution)/shard_map/ppermute | solution.py:211
  6.5 0.0 collective-permute-start.2
  6.5 0.0 collective-permute-done.earlier_ref.refs_0_
  6.5 1.6 %shard_map.55 = (bf16[256,128]{1,0:T(8,128)(2,1)S(1)}, bf16[256,128]{1,0:T(8,128)(2,1)S(1)}, f32[16,128]{1,0:T(8,128)S(1)}) custom-call(s32[4]{0:T(128)} %bitcast.2, bf16[32,4,128]{2,1,0:T(4,128)(2,1)} %confidence_ref.1, bf16[32,4,128]{2,1,0:T(4,128)(2,1)} %ratings_ref.1, bf16[128,128]{1,0:T(8,128)(2,1)} %factors_ref.1, s32[1,32]{1,0:T(1,128)} %bitcast.3, ...), custom_call_target="tpu_custom_call" | custom-call | tf_op jit(solution)/shard_map/pallas_call | solution.py:216
  8.2 1.8 %collective-permute-start.6 = (bf16[256,128]{1,0:T(8,128)(2,1)S(1)}, bf16[256,128]{1,0:T(8,128)(2,1)S(1)}, u32[]{:S(2)}, u32[]{:S(2)}) collective-permute-start(bf16[256,128]{1,0:T(8,128)(2,1)S(1)} %get-tuple-element.9), channel_id=1, source_target_pairs={{0,2},{2,0},{1,3},{3,1},{4,6},{6,4},{5,7},{7,5},{8,10},{10,8},{9,1... | collective-permute-start | bytes 196616 | tf_op jit(solution)/shard_map/ppermute | solution.py:232
  9.9 0.0 collective-permute-start.3
  9.9 0.7 %collective-permute-done.1.refs_1_ = bf16[128,128]{1,0:T(8,128)(2,1)S(1)} collective-permute-done((bf16[128,128]{1,0:T(8,128)(2,1)}, bf16[128,128]{1,0:T(8,128)(2,1)S(1)}, u32[]{:S(2)}, u32[]{:S(2)}) %collective-permute-start.1) | collective-permute-done | bytes 32800 | tf_op jit(solution)/shard_map/ppermute | solution.py:211
  10.6 0.0 collective-permute-start.4
  10.6 0.0 collective-permute-done.2.refs_2_
  10.6 0.5 %collective-permute-start.5 = (bf16[128,128]{1,0:T(8,128)(2,1)S(1)}, bf16[128,128]{1,0:T(8,128)(2,1)S(1)}, u32[]{:S(2)}, u32[]{:S(2)}) collective-permute-start(bf16[128,128]{1,0:T(8,128)(2,1)S(1)} %collective-permute-done.2.refs_2_), channel_id=1, source_target_pairs={{0,1},{1,0},{2,3},{3,2},{4,5},{5,4},{6,7},{7,6},{8,9},{9,8},{10,11... | collective-permute-start | bytes 98312 | tf_op jit(solution)/shard_map/ppermute | solution.py:212
  11.1 0.0 collective-permute-done.3.refs_3_
  11.1 0.7 %collective-permute-done.4.refs_4_ = bf16[128,128]{1,0:T(8,128)(2,1)S(1)} collective-permute-done((bf16[128,128]{1,0:T(8,128)(2,1)S(1)}, bf16[128,128]{1,0:T(8,128)(2,1)S(1)}, u32[]{:S(2)}, u32[]{:S(2)}) %collective-permute-start.4) | collective-permute-done | bytes 32800 | tf_op jit(solution)/shard_map/ppermute | solution.py:212
  11.8 0.2 %collective-permute-done.5.refs_5_ = bf16[128,128]{1,0:T(8,128)(2,1)S(1)} collective-permute-done((bf16[128,128]{1,0:T(8,128)(2,1)S(1)}, bf16[128,128]{1,0:T(8,128)(2,1)S(1)}, u32[]{:S(2)}, u32[]{:S(2)}) %collective-permute-start.5) | collective-permute-done | bytes 32800 | tf_op jit(solution)/shard_map/ppermute | solution.py:212
  12.0 0.5 %collective-permute-done.6.refs_7_ = bf16[256,128]{1,0:T(8,128)(2,1)S(1)} collective-permute-done((bf16[256,128]{1,0:T(8,128)(2,1)S(1)}, bf16[256,128]{1,0:T(8,128)(2,1)S(1)}, u32[]{:S(2)}, u32[]{:S(2)}) %collective-permute-start.6) | collective-permute-done | bytes 65568 | tf_op jit(solution)/shard_map/ppermute | solution.py:232
  12.5 2.1 %shard_map.56 = f32[16,64]{1,0:T(8,128)} custom-call(bf16[128,128]{1,0:T(8,128)(2,1)S(1)} %collective-permute-done.earlier_ref.refs_0_, bf16[128,128]{1,0:T(8,128)(2,1)S(1)} %collective-permute-done.1.refs_1_, bf16[128,128]{1,0:T(8,128)(2,1)S(1)} %collective-permute-done.2.refs_2_, bf16[128,128]{1,0:T(8,128)(2,1)S(1)} %collective-permute-done.3.refs_3_, ...), custom_call_target="tpu_custom_call" | custom-call | tf_op jit(solution)/shard_map/pallas_call | solution.py:233
Async XLA Ops:
  0.0 6.5 %collective-permute-start = (bf16[128,128]{1,0:T(8,128)(2,1)}, bf16[128,128]{1,0:T(8,128)(2,1)S(1)}, u32[]{:S(2)}, u32[]{:S(2)}) collective-permute-start(bf16[128,128]{1,0:T(8,128)(2,1)} %factors_ref.1), channel_id=1, source_target_pairs={{0,6},{2,4},{4,2},{6,0},{8,14},{10,12},{12,10},{14,8},{1,5},{3,7},... | collective-permute-start | bytes 98312 | tf_op jit(solution)/shard_map/ppermute | solution.py:211
  4.0 6.7 %collective-permute-start.1 = (bf16[128,128]{1,0:T(8,128)(2,1)}, bf16[128,128]{1,0:T(8,128)(2,1)S(1)}, u32[]{:S(2)}, u32[]{:S(2)}) collective-permute-start(bf16[128,128]{1,0:T(8,128)(2,1)} %factors_ref.1), channel_id=1, source_target_pairs={{0,10},{2,8},{4,14},{6,12},{8,2},{10,0},{12,6},{14,4},{1,15},{3,13... | collective-permute-start | bytes 98312 | tf_op jit(solution)/shard_map/ppermute | solution.py:211
  6.5 4.1 %collective-permute-start.2 = (bf16[128,128]{1,0:T(8,128)(2,1)}, bf16[128,128]{1,0:T(8,128)(2,1)S(1)}, u32[]{:S(2)}, u32[]{:S(2)}) collective-permute-start(bf16[128,128]{1,0:T(8,128)(2,1)} %factors_ref.1), channel_id=1, source_target_pairs={{0,12},{2,14},{4,0},{6,2},{8,4},{10,6},{12,8},{14,10},{1,9},{3,11}... | collective-permute-start | bytes 98312 | tf_op jit(solution)/shard_map/ppermute | solution.py:211
  8.2 4.3 %collective-permute-start.6 = (bf16[256,128]{1,0:T(8,128)(2,1)S(1)}, bf16[256,128]{1,0:T(8,128)(2,1)S(1)}, u32[]{:S(2)}, u32[]{:S(2)}) collective-permute-start(bf16[256,128]{1,0:T(8,128)(2,1)S(1)} %get-tuple-element.9), channel_id=1, source_target_pairs={{0,2},{2,0},{1,3},{3,1},{4,6},{6,4},{5,7},{7,5},{8,10},{10,8},{9,1... | collective-permute-start | bytes 196616 | tf_op jit(solution)/shard_map/ppermute | solution.py:232
  9.9 1.2 %collective-permute-start.3 = (bf16[128,128]{1,0:T(8,128)(2,1)S(1)}, bf16[128,128]{1,0:T(8,128)(2,1)S(1)}, u32[]{:S(2)}, u32[]{:S(2)}) collective-permute-start(bf16[128,128]{1,0:T(8,128)(2,1)S(1)} %collective-permute-done.earlier_ref.refs_0_), channel_id=1, source_target_pairs={{0,1},{1,0},{2,3},{3,2},{4,5},{5,4},{6,7},{7,6},{8,9},{9,8},{10,11... | collective-permute-start | bytes 98312 | tf_op jit(solution)/shard_map/ppermute | solution.py:212
  10.6 1.2 %collective-permute-start.4 = (bf16[128,128]{1,0:T(8,128)(2,1)S(1)}, bf16[128,128]{1,0:T(8,128)(2,1)S(1)}, u32[]{:S(2)}, u32[]{:S(2)}) collective-permute-start(bf16[128,128]{1,0:T(8,128)(2,1)S(1)} %collective-permute-done.1.refs_1_), channel_id=1, source_target_pairs={{0,1},{1,0},{2,3},{3,2},{4,5},{5,4},{6,7},{7,6},{8,9},{9,8},{10,11... | collective-permute-start | bytes 98312 | tf_op jit(solution)/shard_map/ppermute | solution.py:212
  10.6 1.4 %collective-permute-start.5 = (bf16[128,128]{1,0:T(8,128)(2,1)S(1)}, bf16[128,128]{1,0:T(8,128)(2,1)S(1)}, u32[]{:S(2)}, u32[]{:S(2)}) collective-permute-start(bf16[128,128]{1,0:T(8,128)(2,1)S(1)} %collective-permute-done.2.refs_2_), channel_id=1, source_target_pairs={{0,1},{1,0},{2,3},{3,2},{4,5},{5,4},{6,7},{7,6},{8,9},{9,8},{10,11... | collective-permute-start | bytes 98312 | tf_op jit(solution)/shard_map/ppermute | solution.py:212

commit v5 on v4

--- a/solution.py
+++ b/solution.py
@@ -123,13 +123,16 @@
     weight_ref,
     rating_ref,
     count_ref,
+    flag_ref,
     value_ref,
     arrived,
 ):
     del earlier_ref
     group = lax.axis_index("grp")
-    users, cycle_size, tile_items = confidence_ref.shape
-    owned = users // 2
+    rows, tile_items = confidence_ref.shape
+    owned = ridge_ref.shape[0]
+    users = 2 * owned
+    cycle_size = rows // users
     copies = [
         pltpu.make_async_copy(source, target, arrived.at[number])
         for number, (source, target) in enumerate(
@@ -139,6 +142,7 @@
                 (factors_ref, mine_ref.at[pl.ds(0, tile_items)]),
                 (factors_ref, theirs_ref.at[pl.ds(0, tile_items)]),
                 (counts_ref, count_ref),
+                (flags_ref, flag_ref),
             )
         )
     ]
@@ -146,13 +150,13 @@
         copy.start()
     copies[0].wait()
     copies[1].wait()
-    rows = users * cycle_size
-    weight = weight_ref[...].astype(jnp.float32).reshape(rows, tile_items)
-    rating = rating_ref[...].astype(jnp.float32).reshape(rows, tile_items)
+    copies[5].wait()
+    weight = weight_ref[...].astype(jnp.float32)
+    rating = rating_ref[...].astype(jnp.float32)
     source = lax.rem(lax.broadcasted_iota(jnp.int32, (rows, tile_items), 0), cycle_size)
     flag = jnp.zeros_like(source)
     for number in range(cycle_size):
-        flag = jnp.where(source == number, flags_ref[number], flag)
+        flag = jnp.where(source == number, flag_ref[number], flag)
     weight = jnp.where(flag != 0, weight, 0.0)
     for kind, value in enumerate((weight, weight * rating)):
         value_ref[kind] = value
@@ -163,7 +167,7 @@
                 packet_ref[target] = value_ref[
                     kind, pl.ds(start, owned, stride=cycle_size)
                 ].astype(jnp.bfloat16)
-    for copy in copies[2:]:
+    for copy in copies[2:5]:
         copy.wait()
     user = lax.broadcasted_iota(jnp.int32, (owned, users), 0) + group * owned
     entry = lax.broadcasted_iota(jnp.int32, user.shape, 1)
@@ -199,7 +203,6 @@
 
 
 VMEM = pl.BlockSpec(memory_space=pltpu.VMEM)
-SMEM = pl.BlockSpec(memory_space=pltpu.SMEM)
 HBM = pl.BlockSpec(memory_space=pltpu.HBM)
 
 
@@ -210,20 +213,28 @@
     swap = [(0, 1), (1, 0)]
     direct = [lax.ppermute(item_factors, PLACE, exchange_route(rules)) for rules in EXCHANGES]
     passed = [lax.ppermute(block, "rep", swap) for block in direct]
-    packet_inputs = (pattern[0, :, 0], confidence, ratings, item_factors, counts[None])
+    rows = (users * cycle_size, tile_items)
+    packet_inputs = (
+        pattern[0, :, 0],
+        confidence.reshape(rows),
+        ratings.reshape(rows),
+        item_factors,
+        counts[None],
+    )
     packet = jax.ShapeDtypeStruct((tile_items + 2 * cycle_size * owned, dim), jnp.bfloat16)
     ridge = jax.ShapeDtypeStruct((owned, dim), jnp.float32)
     mine, theirs, ridge = pl.pallas_call(
         packet_kernel,
         out_shape=(packet, packet, ridge),
-        in_specs=[SMEM, HBM, HBM, HBM, HBM, VMEM],
+        in_specs=[HBM] * 5 + [VMEM],
         out_specs=(VMEM, VMEM, VMEM),
         scratch_shapes=[
-            pltpu.VMEM(confidence.shape, jnp.bfloat16),
-            pltpu.VMEM(ratings.shape, jnp.bfloat16),
+            pltpu.VMEM(rows, jnp.bfloat16),
+            pltpu.VMEM(rows, jnp.bfloat16),
             pltpu.VMEM((1, users), jnp.int32),
-            pltpu.VMEM((2, users * cycle_size, tile_items), jnp.float32),
-            pltpu.SemaphoreType.DMA((5,)),
+            pltpu.SMEM((cycle_size,), jnp.int32),
+            pltpu.VMEM((2, *rows), jnp.float32),
+            pltpu.SemaphoreType.DMA((6,)),
         ],
         compiler_params=pltpu.CompilerParams(vmem_limit_bytes=8 * 1024 * 1024),
     )(

time: 14.7 us -> 14.3 us (0.973)
  Pallas kernels: 3.69 us -> 3.05 us
  waiting for transfers between devices: 2.04 us -> 2.29 us
    ppermute x3, waiting for transfers between devices: 0.69 us -> 1.43 us  [chip_shards(): lax.ppermute(item_factors, PLACE, exchange_route(rules))]
    pallas_call x1, Pallas kernels: 1.64 us -> 0.99 us  [chip_shards(): pl.pallas_call(packet_kernel, out_shape=(packet, packet, ridge), in_specs...]
    ppermute x1, waiting for transfers between devices: 0.49 us -> 0.01 us  [chip_shards(): theirs = lax.ppermute(theirs, 'grp', swap)]
  transfers between devices with their start and end apart: 7 -> 7, of which waited for: 4 -> 3; matrix products, arithmetic and copies ran while one was open for 0% -> 0% of each run, Pallas kernels for 11% -> 7%
where the time goes in v5:
time: 14.3 us; the launch traced here: 14.2 us
  starting transfers between devices  8.8 us (62%)
  Pallas kernels  3.05 us (21%)
  waiting for transfers between devices  2.29 us (16%)
    ppermute x3, starting transfers between devices, chip_shards(): lax.ppermute(item_factors, PLACE, exchange_route(rules))  6.51 us
    pallas_call x1, Pallas kernels, chip_shards(): pl.pallas_call(chip_kernel, out_shape=jax.ShapeDtypeStruct((owned, dim //...  2.06 us
    ppermute x1, starting transfers between devices, chip_shards(): theirs = lax.ppermute(theirs, 'grp', swap)  1.77 us
    ppermute x3, waiting for transfers between devices, chip_shards(): lax.ppermute(item_factors, PLACE, exchange_route(rules))  1.43 us
    pallas_call x1, Pallas kernels, chip_shards(): pl.pallas_call(packet_kernel, out_shape=(packet, packet, ridge), in_specs...  0.99 us
    ppermute x3, waiting for transfers between devices, chip_shards(): passed = [lax.ppermute(block, 'rep', swap) for block in direct]  0.86 us
    ppermute x3, starting transfers between devices, chip_shards(): passed = [lax.ppermute(block, 'rep', swap) for block in direct]  0.51 us
  transfers between devices with their start and end apart: 7, of which 3 were waited for; matrix products, arithmetic and copies ran while one was open for 0% of the time, Pallas kernels for 7%

profile of v5, /device:TPU:0, one launch (start us, length us, event | category | flops | bytes accessed | tf_op | source)
XLA Modules:
  0.0 14.2 jit_solution(10933295703940798920)
XLA Ops:
  0.0 4.0 %collective-permute-start = (bf16[128,128]{1,0:T(8,128)(2,1)}, bf16[128,128]{1,0:T(8,128)(2,1)S(1)}, u32[]{:S(2)}, u32[]{:S(2)}) collective-permute-start(bf16[128,128]{1,0:T(8,128)(2,1)} %factors_ref.1), channel_id=1, source_target_pairs={{0,6},{2,4},{4,2},{6,0},{8,14},{10,12},{12,10},{14,8},{1,5},{3,7},... | collective-permute-start | bytes 98312 | tf_op jit(solution)/shard_map/ppermute | solution.py:214
  4.0 2.6 %collective-permute-start.1 = (bf16[128,128]{1,0:T(8,128)(2,1)}, bf16[128,128]{1,0:T(8,128)(2,1)S(1)}, u32[]{:S(2)}, u32[]{:S(2)}) collective-permute-start(bf16[128,128]{1,0:T(8,128)(2,1)} %factors_ref.1), channel_id=1, source_target_pairs={{0,10},{2,8},{4,14},{6,12},{8,2},{10,0},{12,6},{14,4},{1,15},{3,13... | collective-permute-start | bytes 98312 | tf_op jit(solution)/shard_map/ppermute | solution.py:214
  6.5 0.0 collective-permute-start.2
  6.5 0.0 collective-permute-done.earlier_ref.refs_0_
  6.5 1.0 %shard_map.55 = (bf16[256,128]{1,0:T(8,128)(2,1)S(1)}, bf16[256,128]{1,0:T(8,128)(2,1)S(1)}, f32[16,128]{1,0:T(8,128)S(1)}) custom-call(s32[4]{0:T(128)} %bitcast.6, bf16[128,128]{1,0:T(8,128)(2,1)} %bitcast.4, bf16[128,128]{1,0:T(8,128)(2,1)} %bitcast.5, bf16[128,128]{1,0:T(8,128)(2,1)} %factors_ref.1, s32[1,32]{1,0:T(1,128)} %bitcast.7, ...), custom_call_target="tpu_custom_call" | custom-call | tf_op jit(solution)/shard_map/pallas_call | solution.py:226
  7.5 1.8 %collective-permute-start.6 = (bf16[256,128]{1,0:T(8,128)(2,1)S(1)}, bf16[256,128]{1,0:T(8,128)(2,1)S(1)}, u32[]{:S(2)}, u32[]{:S(2)}) collective-permute-start(bf16[256,128]{1,0:T(8,128)(2,1)S(1)} %get-tuple-element.9), channel_id=1, source_target_pairs={{0,2},{2,0},{1,3},{3,1},{4,6},{6,4},{5,7},{7,5},{8,10},{10,8},{9,1... | collective-permute-start | bytes 196616 | tf_op jit(solution)/shard_map/ppermute | solution.py:243
  9.3 0.0 collective-permute-start.3
  9.3 1.4 %collective-permute-done.1.refs_1_ = bf16[128,128]{1,0:T(8,128)(2,1)S(1)} collective-permute-done((bf16[128,128]{1,0:T(8,128)(2,1)}, bf16[128,128]{1,0:T(8,128)(2,1)S(1)}, u32[]{:S(2)}, u32[]{:S(2)}) %collective-permute-start.1) | collective-permute-done | bytes 32800 | tf_op jit(solution)/shard_map/ppermute | solution.py:214
  10.7 0.0 collective-permute-start.4
  10.7 0.0 collective-permute-done.2.refs_2_
  10.7 0.5 %collective-permute-start.5 = (bf16[128,128]{1,0:T(8,128)(2,1)S(1)}, bf16[128,128]{1,0:T(8,128)(2,1)S(1)}, u32[]{:S(2)}, u32[]{:S(2)}) collective-permute-start(bf16[128,128]{1,0:T(8,128)(2,1)S(1)} %collective-permute-done.2.refs_2_), channel_id=1, source_target_pairs={{0,1},{1,0},{2,3},{3,2},{4,5},{5,4},{6,7},{7,6},{8,9},{9,8},{10,11... | collective-permute-start | bytes 98312 | tf_op jit(solution)/shard_map/ppermute | solution.py:215
  11.2 0.0 collective-permute-done.3.refs_3_
  11.2 0.7 %collective-permute-done.4.refs_4_ = bf16[128,128]{1,0:T(8,128)(2,1)S(1)} collective-permute-done((bf16[128,128]{1,0:T(8,128)(2,1)S(1)}, bf16[128,128]{1,0:T(8,128)(2,1)S(1)}, u32[]{:S(2)}, u32[]{:S(2)}) %collective-permute-start.4) | collective-permute-done | bytes 32800 | tf_op jit(solution)/shard_map/ppermute | solution.py:215
  11.9 0.2 %collective-permute-done.5.refs_5_ = bf16[128,128]{1,0:T(8,128)(2,1)S(1)} collective-permute-done((bf16[128,128]{1,0:T(8,128)(2,1)S(1)}, bf16[128,128]{1,0:T(8,128)(2,1)S(1)}, u32[]{:S(2)}, u32[]{:S(2)}) %collective-permute-start.5) | collective-permute-done | bytes 32800 | tf_op jit(solution)/shard_map/ppermute | solution.py:215
  12.1 0.0 collective-permute-done.6.refs_7_
  12.1 2.1 %shard_map.56 = f32[16,64]{1,0:T(8,128)} custom-call(bf16[128,128]{1,0:T(8,128)(2,1)S(1)} %collective-permute-done.earlier_ref.refs_0_, bf16[128,128]{1,0:T(8,128)(2,1)S(1)} %collective-permute-done.1.refs_1_, bf16[128,128]{1,0:T(8,128)(2,1)S(1)} %collective-permute-done.2.refs_2_, bf16[128,128]{1,0:T(8,128)(2,1)S(1)} %collective-permute-done.3.refs_3_, ...), custom_call_target="tpu_custom_call" | custom-call | tf_op jit(solution)/shard_map/pallas_call | solution.py:244
Async XLA Ops:
  0.0 6.5 %collective-permute-start = (bf16[128,128]{1,0:T(8,128)(2,1)}, bf16[128,128]{1,0:T(8,128)(2,1)S(1)}, u32[]{:S(2)}, u32[]{:S(2)}) collective-permute-start(bf16[128,128]{1,0:T(8,128)(2,1)} %factors_ref.1), channel_id=1, source_target_pairs={{0,6},{2,4},{4,2},{6,0},{8,14},{10,12},{12,10},{14,8},{1,5},{3,7},... | collective-permute-start | bytes 98312 | tf_op jit(solution)/shard_map/ppermute | solution.py:214
  4.0 6.8 %collective-permute-start.1 = (bf16[128,128]{1,0:T(8,128)(2,1)}, bf16[128,128]{1,0:T(8,128)(2,1)S(1)}, u32[]{:S(2)}, u32[]{:S(2)}) collective-permute-start(bf16[128,128]{1,0:T(8,128)(2,1)} %factors_ref.1), channel_id=1, source_target_pairs={{0,10},{2,8},{4,14},{6,12},{8,2},{10,0},{12,6},{14,4},{1,15},{3,13... | collective-permute-start | bytes 98312 | tf_op jit(solution)/shard_map/ppermute | solution.py:214
  6.5 4.2 %collective-permute-start.2 = (bf16[128,128]{1,0:T(8,128)(2,1)}, bf16[128,128]{1,0:T(8,128)(2,1)S(1)}, u32[]{:S(2)}, u32[]{:S(2)}) collective-permute-start(bf16[128,128]{1,0:T(8,128)(2,1)} %factors_ref.1), channel_id=1, source_target_pairs={{0,12},{2,14},{4,0},{6,2},{8,4},{10,6},{12,8},{14,10},{1,9},{3,11}... | collective-permute-start | bytes 98312 | tf_op jit(solution)/shard_map/ppermute | solution.py:214
  7.5 4.6 %collective-permute-start.6 = (bf16[256,128]{1,0:T(8,128)(2,1)S(1)}, bf16[256,128]{1,0:T(8,128)(2,1)S(1)}, u32[]{:S(2)}, u32[]{:S(2)}) collective-permute-start(bf16[256,128]{1,0:T(8,128)(2,1)S(1)} %get-tuple-element.9), channel_id=1, source_target_pairs={{0,2},{2,0},{1,3},{3,1},{4,6},{6,4},{5,7},{7,5},{8,10},{10,8},{9,1... | collective-permute-start | bytes 196616 | tf_op jit(solution)/shard_map/ppermute | solution.py:243
  9.3 1.9 %collective-permute-start.3 = (bf16[128,128]{1,0:T(8,128)(2,1)S(1)}, bf16[128,128]{1,0:T(8,128)(2,1)S(1)}, u32[]{:S(2)}, u32[]{:S(2)}) collective-permute-start(bf16[128,128]{1,0:T(8,128)(2,1)S(1)} %collective-permute-done.earlier_ref.refs_0_), channel_id=1, source_target_pairs={{0,1},{1,0},{2,3},{3,2},{4,5},{5,4},{6,7},{7,6},{8,9},{9,8},{10,11... | collective-permute-start | bytes 98312 | tf_op jit(solution)/shard_map/ppermute | solution.py:215
  10.7 1.2 %collective-permute-start.4 = (bf16[128,128]{1,0:T(8,128)(2,1)S(1)}, bf16[128,128]{1,0:T(8,128)(2,1)S(1)}, u32[]{:S(2)}, u32[]{:S(2)}) collective-permute-start(bf16[128,128]{1,0:T(8,128)(2,1)S(1)} %collective-permute-done.1.refs_1_), channel_id=1, source_target_pairs={{0,1},{1,0},{2,3},{3,2},{4,5},{5,4},{6,7},{7,6},{8,9},{9,8},{10,11... | collective-permute-start | bytes 98312 | tf_op jit(solution)/shard_map/ppermute | solution.py:215
  10.7 1.4 %collective-permute-start.5 = (bf16[128,128]{1,0:T(8,128)(2,1)S(1)}, bf16[128,128]{1,0:T(8,128)(2,1)S(1)}, u32[]{:S(2)}, u32[]{:S(2)}) collective-permute-start(bf16[128,128]{1,0:T(8,128)(2,1)S(1)} %collective-permute-done.2.refs_2_), channel_id=1, source_target_pairs={{0,1},{1,0},{2,3},{3,2},{4,5},{5,4},{6,7},{7,6},{8,9},{9,8},{10,11... | collective-permute-start | bytes 98312 | tf_op jit(solution)/shard_map/ppermute | solution.py:215

commit v6 on v5

--- a/solution.py
+++ b/solution.py
@@ -16,10 +16,11 @@
 PLACE = ("blk", "grp", "rep")
 ADD, FLIP = "add", "flip"
 EXCHANGES = (
-    ((FLIP, 1, 1), (ADD, 1, 0)),
-    ((FLIP, 2, 1), (FLIP, 3, 1)),
-    ((ADD, 3, 0), (ADD, 2, 0)),
+    ((FLIP, 1, 1), (ADD, 1, 0), 1),
+    ((FLIP, 2, 1), (FLIP, 3, 1), 0),
+    ((ADD, 3, 0), (ADD, 2, 0), 0),
 )
+PACKET_ACROSS = 1
 
 
 def stepped(change, position, steps):
@@ -28,12 +29,16 @@
 
 def exchange_route(rules):
     route = []
+    *rules, across = rules
     for core, (change, steps, other) in enumerate(rules):
         for position in range(4):
             for group in range(2):
                 target = stepped(change, position, steps)
                 route.append(
-                    ((position * 2 + group) * 2 + core, (target * 2 + (group ^ other)) * 2 + core)
+                    (
+                        (position * 2 + group) * 2 + core,
+                        (target * 2 + (group ^ other)) * 2 + (core ^ across),
+                    )
                 )
     return route
 
@@ -182,7 +187,9 @@
     slots, tile_items, dim = held.shape
     owned, cycle_size = out_ref.shape[0], slots // 2
     for number, rules in enumerate(EXCHANGES):
+        *rules, across = rules
         places = [source_slot(rule, position) for rule in rules]
+        places = places[::-1] if across else places
         direct, passed = block_refs[number], block_refs[len(EXCHANGES) + number]
         held[jnp.where(core == 0, places[0], places[1])] = direct[...]
         held[jnp.where(core == 0, places[1], places[0])] = passed[...]
@@ -240,7 +247,7 @@
     )(
         *(pltpu.with_memory_space_constraint(array, pltpu.HBM) for array in packet_inputs), direct[0]
     )
-    theirs = lax.ppermute(theirs, "grp", swap)
+    theirs = lax.ppermute(theirs, PLACE, exchange_route((*((ADD, 0, 1),) * 2, PACKET_ACROSS)))
     return pl.pallas_call(
         chip_kernel,
         out_shape=jax.ShapeDtypeStruct((owned, dim // 2), jnp.float32),

time: 14.3 us -> 13.8 us (0.965)
  waiting for transfers between devices: 2.29 us -> 1.76 us
    ppermute x3, starting transfers between devices: 0.51 us -> 1.87 us  [chip_shards(): passed = [lax.ppermute(block, 'rep', swap) for block in direct]]
    ppermute x1, starting transfers between devices: 1.77 us -> 0.57 us  [chip_shards(): lax.ppermute(theirs, PLACE, exchange_route((*((ADD, 0, 1),) * 2, PACKET_A...]
    ppermute x3, waiting for transfers between devices: 1.43 us -> 0.84 us  [chip_shards(): lax.ppermute(item_factors, PLACE, exchange_route(rules))]
    ppermute x3, starting transfers between devices: 6.51 us -> 6.31 us  [chip_shards(): lax.ppermute(item_factors, PLACE, exchange_route(rules))]
  transfers between devices with their start and end apart: 7 -> 7, of which waited for: 3 -> 4; matrix products, arithmetic and copies ran while one was open for 0% -> 0% of each run, Pallas kernels for 7% -> 7%
where the time goes in v6:
time: 13.8 us; the launch traced here: 13.6 us
  starting transfers between devices  8.75 us (63%)
  Pallas kernels  3.04 us (22%)
  waiting for transfers between devices  1.76 us (13%)
    ppermute x3, starting transfers between devices, chip_shards(): lax.ppermute(item_factors, PLACE, exchange_route(rules))  6.31 us
    pallas_call x1, Pallas kernels, chip_shards(): pl.pallas_call(chip_kernel, out_shape=jax.ShapeDtypeStruct((owned, dim //...  2.06 us
    ppermute x3, starting transfers between devices, chip_shards(): passed = [lax.ppermute(block, 'rep', swap) for block in direct]  1.87 us
    pallas_call x1, Pallas kernels, chip_shards(): pl.pallas_call(packet_kernel, out_shape=(packet, packet, ridge), in_specs...  0.99 us
    ppermute x3, waiting for transfers between devices, chip_shards(): passed = [lax.ppermute(block, 'rep', swap) for block in direct]  0.92 us
    ppermute x3, waiting for transfers between devices, chip_shards(): lax.ppermute(item_factors, PLACE, exchange_route(rules))  0.84 us
    ppermute x1, starting transfers between devices, chip_shards(): lax.ppermute(theirs, PLACE, exchange_route((*((ADD, 0, 1),) * 2, PACKET_A...  0.57 us
  transfers between devices with their start and end apart: 7, of which 4 were waited for; matrix products, arithmetic and copies ran while one was open for 0% of the time, Pallas kernels for 7%

profile of v6, /device:TPU:0, one launch (start us, length us, event | category | flops | bytes accessed | tf_op | source)
XLA Modules:
  0.0 13.6 jit_solution(11799919008278562685)
XLA Ops:
  0.0 3.4 %collective-permute-start = (bf16[128,128]{1,0:T(8,128)(2,1)}, bf16[128,128]{1,0:T(8,128)(2,1)S(1)}, u32[]{:S(2)}, u32[]{:S(2)}) collective-permute-start(bf16[128,128]{1,0:T(8,128)(2,1)} %factors_ref.1), channel_id=1, source_target_pairs={{0,7},{2,5},{4,3},{6,1},{8,15},{10,13},{12,11},{14,9},{1,4},{3,6},... | collective-permute-start | bytes 98312 | tf_op jit(solution)/shard_map/ppermute | solution.py:221
  3.4 2.6 %collective-permute-start.1 = (bf16[128,128]{1,0:T(8,128)(2,1)}, bf16[128,128]{1,0:T(8,128)(2,1)S(1)}, u32[]{:S(2)}, u32[]{:S(2)}) collective-permute-start(bf16[128,128]{1,0:T(8,128)(2,1)} %factors_ref.1), channel_id=1, source_target_pairs={{0,10},{2,8},{4,14},{6,12},{8,2},{10,0},{12,6},{14,4},{1,15},{3,13... | collective-permute-start | bytes 98312 | tf_op jit(solution)/shard_map/ppermute | solution.py:221
  6.0 0.4 %collective-permute-start.2 = (bf16[128,128]{1,0:T(8,128)(2,1)}, bf16[128,128]{1,0:T(8,128)(2,1)S(1)}, u32[]{:S(2)}, u32[]{:S(2)}) collective-permute-start(bf16[128,128]{1,0:T(8,128)(2,1)} %factors_ref.1), channel_id=1, source_target_pairs={{0,12},{2,14},{4,0},{6,2},{8,4},{10,6},{12,8},{14,10},{1,9},{3,11}... | collective-permute-start | bytes 98312 | tf_op jit(solution)/shard_map/ppermute | solution.py:221
  6.3 0.0 collective-permute-done.earlier_ref.refs_0_
  6.3 1.0 %shard_map.55 = (bf16[256,128]{1,0:T(8,128)(2,1)S(1)}, bf16[256,128]{1,0:T(8,128)(2,1)S(1)}, f32[16,128]{1,0:T(8,128)S(1)}) custom-call(s32[4]{0:T(128)} %bitcast.6, bf16[128,128]{1,0:T(8,128)(2,1)} %bitcast.4, bf16[128,128]{1,0:T(8,128)(2,1)} %bitcast.5, bf16[128,128]{1,0:T(8,128)(2,1)} %factors_ref.1, s32[1,32]{1,0:T(1,128)} %bitcast.7, ...), custom_call_target="tpu_custom_call" | custom-call | tf_op jit(solution)/shard_map/pallas_call | solution.py:233
  7.3 0.6 %collective-permute-start.6 = (bf16[256,128]{1,0:T(8,128)(2,1)S(1)}, bf16[256,128]{1,0:T(8,128)(2,1)S(1)}, u32[]{:S(2)}, u32[]{:S(2)}) collective-permute-start(bf16[256,128]{1,0:T(8,128)(2,1)S(1)} %get-tuple-element.9), channel_id=1, source_target_pairs={{0,3},{2,1},{4,7},{6,5},{8,11},{10,9},{12,15},{14,13},{1,2},{3,0},... | collective-permute-start | bytes 196616 | tf_op jit(solution)/shard_map/ppermute | solution.py:250
  7.9 1.6 %collective-permute-start.3 = (bf16[128,128]{1,0:T(8,128)(2,1)S(1)}, bf16[128,128]{1,0:T(8,128)(2,1)S(1)}, u32[]{:S(2)}, u32[]{:S(2)}) collective-permute-start(bf16[128,128]{1,0:T(8,128)(2,1)S(1)} %collective-permute-done.earlier_ref.refs_0_), channel_id=1, source_target_pairs={{0,1},{1,0},{2,3},{3,2},{4,5},{5,4},{6,7},{7,6},{8,9},{9,8},{10,11... | collective-permute-start | bytes 98312 | tf_op jit(solution)/shard_map/ppermute | solution.py:222
  9.5 0.6 %collective-permute-done.1.refs_1_ = bf16[128,128]{1,0:T(8,128)(2,1)S(1)} collective-permute-done((bf16[128,128]{1,0:T(8,128)(2,1)}, bf16[128,128]{1,0:T(8,128)(2,1)S(1)}, u32[]{:S(2)}, u32[]{:S(2)}) %collective-permute-start.1) | collective-permute-done | bytes 32800 | tf_op jit(solution)/shard_map/ppermute | solution.py:221
  10.0 0.0 collective-permute-start.4
  10.0 0.3 %collective-permute-done.2.refs_2_ = bf16[128,128]{1,0:T(8,128)(2,1)S(1)} collective-permute-done((bf16[128,128]{1,0:T(8,128)(2,1)}, bf16[128,128]{1,0:T(8,128)(2,1)S(1)}, u32[]{:S(2)}, u32[]{:S(2)}) %collective-permute-start.2) | collective-permute-done | bytes 32800 | tf_op jit(solution)/shard_map/ppermute | solution.py:221
  10.3 0.3 %collective-permute-start.5 = (bf16[128,128]{1,0:T(8,128)(2,1)S(1)}, bf16[128,128]{1,0:T(8,128)(2,1)S(1)}, u32[]{:S(2)}, u32[]{:S(2)}) collective-permute-start(bf16[128,128]{1,0:T(8,128)(2,1)S(1)} %collective-permute-done.2.refs_2_), channel_id=1, source_target_pairs={{0,1},{1,0},{2,3},{3,2},{4,5},{5,4},{6,7},{7,6},{8,9},{9,8},{10,11... | collective-permute-start | bytes 98312 | tf_op jit(solution)/shard_map/ppermute | solution.py:222
  10.6 0.0 collective-permute-done.3.refs_3_
  10.6 0.6 %collective-permute-done.4.refs_4_ = bf16[128,128]{1,0:T(8,128)(2,1)S(1)} collective-permute-done((bf16[128,128]{1,0:T(8,128)(2,1)S(1)}, bf16[128,128]{1,0:T(8,128)(2,1)S(1)}, u32[]{:S(2)}, u32[]{:S(2)}) %collective-permute-start.4) | collective-permute-done | bytes 32800 | tf_op jit(solution)/shard_map/ppermute | solution.py:222
  11.2 0.3 %collective-permute-done.5.refs_5_ = bf16[128,128]{1,0:T(8,128)(2,1)S(1)} collective-permute-done((bf16[128,128]{1,0:T(8,128)(2,1)S(1)}, bf16[128,128]{1,0:T(8,128)(2,1)S(1)}, u32[]{:S(2)}, u32[]{:S(2)}) %collective-permute-start.5) | collective-permute-done | bytes 32800 | tf_op jit(solution)/shard_map/ppermute | solution.py:222
  11.5 0.0 collective-permute-done.6.refs_7_
  11.5 2.1 %shard_map.56 = f32[16,64]{1,0:T(8,128)} custom-call(bf16[128,128]{1,0:T(8,128)(2,1)S(1)} %collective-permute-done.earlier_ref.refs_0_, bf16[128,128]{1,0:T(8,128)(2,1)S(1)} %collective-permute-done.1.refs_1_, bf16[128,128]{1,0:T(8,128)(2,1)S(1)} %collective-permute-done.2.refs_2_, bf16[128,128]{1,0:T(8,128)(2,1)S(1)} %collective-permute-done.3.refs_3_, ...), custom_call_target="tpu_custom_call" | custom-call | tf_op jit(solution)/shard_map/pallas_call | solution.py:251
Async XLA Ops:
  0.0 6.3 %collective-permute-start = (bf16[128,128]{1,0:T(8,128)(2,1)}, bf16[128,128]{1,0:T(8,128)(2,1)S(1)}, u32[]{:S(2)}, u32[]{:S(2)}) collective-permute-start(bf16[128,128]{1,0:T(8,128)(2,1)} %factors_ref.1), channel_id=1, source_target_pairs={{0,7},{2,5},{4,3},{6,1},{8,15},{10,13},{12,11},{14,9},{1,4},{3,6},... | collective-permute-start | bytes 98312 | tf_op jit(solution)/shard_map/ppermute | solution.py:221
  3.4 6.6 %collective-permute-start.1 = (bf16[128,128]{1,0:T(8,128)(2,1)}, bf16[128,128]{1,0:T(8,128)(2,1)S(1)}, u32[]{:S(2)}, u32[]{:S(2)}) collective-permute-start(bf16[128,128]{1,0:T(8,128)(2,1)} %factors_ref.1), channel_id=1, source_target_pairs={{0,10},{2,8},{4,14},{6,12},{8,2},{10,0},{12,6},{14,4},{1,15},{3,13... | collective-permute-start | bytes 98312 | tf_op jit(solution)/shard_map/ppermute | solution.py:221
  6.0 4.4 %collective-permute-start.2 = (bf16[128,128]{1,0:T(8,128)(2,1)}, bf16[128,128]{1,0:T(8,128)(2,1)S(1)}, u32[]{:S(2)}, u32[]{:S(2)}) collective-permute-start(bf16[128,128]{1,0:T(8,128)(2,1)} %factors_ref.1), channel_id=1, source_target_pairs={{0,12},{2,14},{4,0},{6,2},{8,4},{10,6},{12,8},{14,10},{1,9},{3,11}... | collective-permute-start | bytes 98312 | tf_op jit(solution)/shard_map/ppermute | solution.py:221
  7.3 4.2 %collective-permute-start.6 = (bf16[256,128]{1,0:T(8,128)(2,1)S(1)}, bf16[256,128]{1,0:T(8,128)(2,1)S(1)}, u32[]{:S(2)}, u32[]{:S(2)}) collective-permute-start(bf16[256,128]{1,0:T(8,128)(2,1)S(1)} %get-tuple-element.9), channel_id=1, source_target_pairs={{0,3},{2,1},{4,7},{6,5},{8,11},{10,9},{12,15},{14,13},{1,2},{3,0},... | collective-permute-start | bytes 196616 | tf_op jit(solution)/shard_map/ppermute | solution.py:250
  7.9 2.7 %collective-permute-start.3 = (bf16[128,128]{1,0:T(8,128)(2,1)S(1)}, bf16[128,128]{1,0:T(8,128)(2,1)S(1)}, u32[]{:S(2)}, u32[]{:S(2)}) collective-permute-start(bf16[128,128]{1,0:T(8,128)(2,1)S(1)} %collective-permute-done.earlier_ref.refs_0_), channel_id=1, source_target_pairs={{0,1},{1,0},{2,3},{3,2},{4,5},{5,4},{6,7},{7,6},{8,9},{9,8},{10,11... | collective-permute-start | bytes 98312 | tf_op jit(solution)/shard_map/ppermute | solution.py:222
  10.0 1.2 %collective-permute-start.4 = (bf16[128,128]{1,0:T(8,128)(2,1)S(1)}, bf16[128,128]{1,0:T(8,128)(2,1)S(1)}, u32[]{:S(2)}, u32[]{:S(2)}) collective-permute-start(bf16[128,128]{1,0:T(8,128)(2,1)S(1)} %collective-permute-done.1.refs_1_), channel_id=1, source_target_pairs={{0,1},{1,0},{2,3},{3,2},{4,5},{5,4},{6,7},{7,6},{8,9},{9,8},{10,11... | collective-permute-start | bytes 98312 | tf_op jit(solution)/shard_map/ppermute | solution.py:222
  10.3 1.2 %collective-permute-start.5 = (bf16[128,128]{1,0:T(8,128)(2,1)S(1)}, bf16[128,128]{1,0:T(8,128)(2,1)S(1)}, u32[]{:S(2)}, u32[]{:S(2)}) collective-permute-start(bf16[128,128]{1,0:T(8,128)(2,1)S(1)} %collective-permute-done.2.refs_2_), channel_id=1, source_target_pairs={{0,1},{1,0},{2,3},{3,2},{4,5},{5,4},{6,7},{7,6},{8,9},{9,8},{10,11... | collective-permute-start | bytes 98312 | tf_op jit(solution)/shard_map/ppermute | solution.py:222

commit v7 on v6

--- a/solution.py
+++ b/solution.py
@@ -16,9 +16,9 @@
 PLACE = ("blk", "grp", "rep")
 ADD, FLIP = "add", "flip"
 EXCHANGES = (
-    ((FLIP, 1, 1), (ADD, 1, 0), 1),
-    ((FLIP, 2, 1), (FLIP, 3, 1), 0),
-    ((ADD, 3, 0), (ADD, 2, 0), 0),
+    ((FLIP, 2, 1), (ADD, 1, 0), 1),
+    ((FLIP, 1, 1), (FLIP, 3, 1), 0),
+    ((ADD, 2, 0), (ADD, 3, 0), 1),
 )
 PACKET_ACROSS = 1
 

time: 13.8 us -> 13.6 us (0.986)
  waiting for transfers between devices: 1.76 us -> 0.87 us
  starting transfers between devices: 8.75 us -> 9.49 us
    ppermute x1, starting transfers between devices: 0.57 us -> 1.64 us  [chip_shards(): lax.ppermute(theirs, PLACE, exchange_route((*((ADD, 0, 1),) * 2, PACKET_A...]
    ppermute x3, waiting for transfers between devices: 0.84 us -> 0.01 us  [chip_shards(): lax.ppermute(item_factors, PLACE, exchange_route(rules))]
    ppermute x3, starting transfers between devices: 1.87 us -> 1.42 us  [chip_shards(): passed = [lax.ppermute(block, 'rep', swap) for block in direct]]
  transfers between devices with their start and end apart: 7 -> 7, of which waited for: 4 -> 2; matrix products, arithmetic and copies ran while one was open for 0% -> 0% of each run, Pallas kernels for 7% -> 7%
where the time goes in v7:
time: 13.6 us; the launch traced here: 13.4 us
  starting transfers between devices  9.49 us (70%)
  Pallas kernels  3.04 us (22%)
  waiting for transfers between devices  0.87 us (6%)
    ppermute x3, starting transfers between devices, chip_shards(): lax.ppermute(item_factors, PLACE, exchange_route(rules))  6.43 us
    pallas_call x1, Pallas kernels, chip_shards(): pl.pallas_call(chip_kernel, out_shape=jax.ShapeDtypeStruct((owned, dim //...  2.06 us
    ppermute x1, starting transfers between devices, chip_shards(): lax.ppermute(theirs, PLACE, exchange_route((*((ADD, 0, 1),) * 2, PACKET_A...  1.64 us
    ppermute x3, starting transfers between devices, chip_shards(): passed = [lax.ppermute(block, 'rep', swap) for block in direct]  1.42 us
    pallas_call x1, Pallas kernels, chip_shards(): pl.pallas_call(packet_kernel, out_shape=(packet, packet, ridge), in_specs...  0.99 us
    ppermute x3, waiting for transfers between devices, chip_shards(): passed = [lax.ppermute(block, 'rep', swap) for block in direct]  0.86 us
  transfers between devices with their start and end apart: 7, of which 2 were waited for; matrix products, arithmetic and copies ran while one was open for 0% of the time, Pallas kernels for 7%

profile of v7, /device:TPU:0, one launch (start us, length us, event | category | flops | bytes accessed | tf_op | source)
XLA Modules:
  0.0 13.4 jit_solution(3697099295933968866)
XLA Ops:
  0.0 4.4 %collective-permute-start = (bf16[128,128]{1,0:T(8,128)(2,1)}, bf16[128,128]{1,0:T(8,128)(2,1)S(1)}, u32[]{:S(2)}, u32[]{:S(2)}) collective-permute-start(bf16[128,128]{1,0:T(8,128)(2,1)} %factors_ref.1), channel_id=1, source_target_pairs={{0,11},{2,9},{4,15},{6,13},{8,3},{10,1},{12,7},{14,5},{1,4},{3,6},... | collective-permute-start | bytes 98312 | tf_op jit(solution)/shard_map/ppermute | solution.py:221
  4.4 1.5 %collective-permute-start.1 = (bf16[128,128]{1,0:T(8,128)(2,1)}, bf16[128,128]{1,0:T(8,128)(2,1)S(1)}, u32[]{:S(2)}, u32[]{:S(2)}) collective-permute-start(bf16[128,128]{1,0:T(8,128)(2,1)} %factors_ref.1), channel_id=1, source_target_pairs={{0,6},{2,4},{4,2},{6,0},{8,14},{10,12},{12,10},{14,8},{1,15},{3,13... | collective-permute-start | bytes 98312 | tf_op jit(solution)/shard_map/ppermute | solution.py:221
  6.0 0.5 %collective-permute-start.2 = (bf16[128,128]{1,0:T(8,128)(2,1)}, bf16[128,128]{1,0:T(8,128)(2,1)S(1)}, u32[]{:S(2)}, u32[]{:S(2)}) collective-permute-start(bf16[128,128]{1,0:T(8,128)(2,1)} %factors_ref.1), channel_id=1, source_target_pairs={{0,9},{2,11},{4,13},{6,15},{8,1},{10,3},{12,5},{14,7},{1,12},{3,14... | collective-permute-start | bytes 98312 | tf_op jit(solution)/shard_map/ppermute | solution.py:221
  6.4 0.0 collective-permute-done.earlier_ref.refs_0_
  6.4 1.0 %shard_map.55 = (bf16[256,128]{1,0:T(8,128)(2,1)S(1)}, bf16[256,128]{1,0:T(8,128)(2,1)S(1)}, f32[16,128]{1,0:T(8,128)S(1)}) custom-call(s32[4]{0:T(128)} %bitcast.6, bf16[128,128]{1,0:T(8,128)(2,1)} %bitcast.4, bf16[128,128]{1,0:T(8,128)(2,1)} %bitcast.5, bf16[128,128]{1,0:T(8,128)(2,1)} %factors_ref.1, s32[1,32]{1,0:T(1,128)} %bitcast.7, ...), custom_call_target="tpu_custom_call" | custom-call | tf_op jit(solution)/shard_map/pallas_call | solution.py:233
  7.4 1.6 %collective-permute-start.6 = (bf16[256,128]{1,0:T(8,128)(2,1)S(1)}, bf16[256,128]{1,0:T(8,128)(2,1)S(1)}, u32[]{:S(2)}, u32[]{:S(2)}) collective-permute-start(bf16[256,128]{1,0:T(8,128)(2,1)S(1)} %get-tuple-element.9), channel_id=1, source_target_pairs={{0,3},{2,1},{4,7},{6,5},{8,11},{10,9},{12,15},{14,13},{1,2},{3,0},... | collective-permute-start | bytes 196616 | tf_op jit(solution)/shard_map/ppermute | solution.py:250
  9.1 0.4 %collective-permute-start.3 = (bf16[128,128]{1,0:T(8,128)(2,1)S(1)}, bf16[128,128]{1,0:T(8,128)(2,1)S(1)}, u32[]{:S(2)}, u32[]{:S(2)}) collective-permute-start(bf16[128,128]{1,0:T(8,128)(2,1)S(1)} %collective-permute-done.earlier_ref.refs_0_), channel_id=1, source_target_pairs={{0,1},{1,0},{2,3},{3,2},{4,5},{5,4},{6,7},{7,6},{8,9},{9,8},{10,11... | collective-permute-start | bytes 98312 | tf_op jit(solution)/shard_map/ppermute | solution.py:222
  9.5 0.0 collective-permute-done.1.refs_1_
  9.5 0.1 collective-permute-start.4
  9.6 0.0 collective-permute-done.2.refs_2_
  9.6 0.9 %collective-permute-start.5 = (bf16[128,128]{1,0:T(8,128)(2,1)S(1)}, bf16[128,128]{1,0:T(8,128)(2,1)S(1)}, u32[]{:S(2)}, u32[]{:S(2)}) collective-permute-start(bf16[128,128]{1,0:T(8,128)(2,1)S(1)} %collective-permute-done.2.refs_2_), channel_id=1, source_target_pairs={{0,1},{1,0},{2,3},{3,2},{4,5},{5,4},{6,7},{7,6},{8,9},{9,8},{10,11... | collective-permute-start | bytes 98312 | tf_op jit(solution)/shard_map/ppermute | solution.py:222
  10.5 0.0 collective-permute-done.3.refs_3_
  10.5 0.2 %collective-permute-done.4.refs_4_ = bf16[128,128]{1,0:T(8,128)(2,1)S(1)} collective-permute-done((bf16[128,128]{1,0:T(8,128)(2,1)S(1)}, bf16[128,128]{1,0:T(8,128)(2,1)S(1)}, u32[]{:S(2)}, u32[]{:S(2)}) %collective-permute-start.4) | collective-permute-done | bytes 32800 | tf_op jit(solution)/shard_map/ppermute | solution.py:222
  10.7 0.7 %collective-permute-done.5.refs_5_ = bf16[128,128]{1,0:T(8,128)(2,1)S(1)} collective-permute-done((bf16[128,128]{1,0:T(8,128)(2,1)S(1)}, bf16[128,128]{1,0:T(8,128)(2,1)S(1)}, u32[]{:S(2)}, u32[]{:S(2)}) %collective-permute-start.5) | collective-permute-done | bytes 32800 | tf_op jit(solution)/shard_map/ppermute | solution.py:222
  11.4 0.0 collective-permute-done.6.refs_7_
  11.4 2.1 %shard_map.56 = f32[16,64]{1,0:T(8,128)} custom-call(bf16[128,128]{1,0:T(8,128)(2,1)S(1)} %collective-permute-done.earlier_ref.refs_0_, bf16[128,128]{1,0:T(8,128)(2,1)S(1)} %collective-permute-done.1.refs_1_, bf16[128,128]{1,0:T(8,128)(2,1)S(1)} %collective-permute-done.2.refs_2_, bf16[128,128]{1,0:T(8,128)(2,1)S(1)} %collective-permute-done.3.refs_3_, ...), custom_call_target="tpu_custom_call" | custom-call | tf_op jit(solution)/shard_map/pallas_call | solution.py:251
Async XLA Ops:
  0.0 6.4 %collective-permute-start = (bf16[128,128]{1,0:T(8,128)(2,1)}, bf16[128,128]{1,0:T(8,128)(2,1)S(1)}, u32[]{:S(2)}, u32[]{:S(2)}) collective-permute-start(bf16[128,128]{1,0:T(8,128)(2,1)} %factors_ref.1), channel_id=1, source_target_pairs={{0,11},{2,9},{4,15},{6,13},{8,3},{10,1},{12,7},{14,5},{1,4},{3,6},... | collective-permute-start | bytes 98312 | tf_op jit(solution)/shard_map/ppermute | solution.py:221
  4.4 5.1 %collective-permute-start.1 = (bf16[128,128]{1,0:T(8,128)(2,1)}, bf16[128,128]{1,0:T(8,128)(2,1)S(1)}, u32[]{:S(2)}, u32[]{:S(2)}) collective-permute-start(bf16[128,128]{1,0:T(8,128)(2,1)} %factors_ref.1), channel_id=1, source_target_pairs={{0,6},{2,4},{4,2},{6,0},{8,14},{10,12},{12,10},{14,8},{1,15},{3,13... | collective-permute-start | bytes 98312 | tf_op jit(solution)/shard_map/ppermute | solution.py:221
  6.0 3.6 %collective-permute-start.2 = (bf16[128,128]{1,0:T(8,128)(2,1)}, bf16[128,128]{1,0:T(8,128)(2,1)S(1)}, u32[]{:S(2)}, u32[]{:S(2)}) collective-permute-start(bf16[128,128]{1,0:T(8,128)(2,1)} %factors_ref.1), channel_id=1, source_target_pairs={{0,9},{2,11},{4,13},{6,15},{8,1},{10,3},{12,5},{14,7},{1,12},{3,14... | collective-permute-start | bytes 98312 | tf_op jit(solution)/shard_map/ppermute | solution.py:221
  7.4 3.9 %collective-permute-start.6 = (bf16[256,128]{1,0:T(8,128)(2,1)S(1)}, bf16[256,128]{1,0:T(8,128)(2,1)S(1)}, u32[]{:S(2)}, u32[]{:S(2)}) collective-permute-start(bf16[256,128]{1,0:T(8,128)(2,1)S(1)} %get-tuple-element.9), channel_id=1, source_target_pairs={{0,3},{2,1},{4,7},{6,5},{8,11},{10,9},{12,15},{14,13},{1,2},{3,0},... | collective-permute-start | bytes 196616 | tf_op jit(solution)/shard_map/ppermute | solution.py:250
  9.1 1.4 %collective-permute-start.3 = (bf16[128,128]{1,0:T(8,128)(2,1)S(1)}, bf16[128,128]{1,0:T(8,128)(2,1)S(1)}, u32[]{:S(2)}, u32[]{:S(2)}) collective-permute-start(bf16[128,128]{1,0:T(8,128)(2,1)S(1)} %collective-permute-done.earlier_ref.refs_0_), channel_id=1, source_target_pairs={{0,1},{1,0},{2,3},{3,2},{4,5},{5,4},{6,7},{7,6},{8,9},{9,8},{10,11... | collective-permute-start | bytes 98312 | tf_op jit(solution)/shard_map/ppermute | solution.py:222
  9.5 1.2 %collective-permute-start.4 = (bf16[128,128]{1,0:T(8,128)(2,1)S(1)}, bf16[128,128]{1,0:T(8,128)(2,1)S(1)}, u32[]{:S(2)}, u32[]{:S(2)}) collective-permute-start(bf16[128,128]{1,0:T(8,128)(2,1)S(1)} %collective-permute-done.1.refs_1_), channel_id=1, source_target_pairs={{0,1},{1,0},{2,3},{3,2},{4,5},{5,4},{6,7},{7,6},{8,9},{9,8},{10,11... | collective-permute-start | bytes 98312 | tf_op jit(solution)/shard_map/ppermute | solution.py:222
  9.6 1.8 %collective-permute-start.5 = (bf16[128,128]{1,0:T(8,128)(2,1)S(1)}, bf16[128,128]{1,0:T(8,128)(2,1)S(1)}, u32[]{:S(2)}, u32[]{:S(2)}) collective-permute-start(bf16[128,128]{1,0:T(8,128)(2,1)S(1)} %collective-permute-done.2.refs_2_), channel_id=1, source_target_pairs={{0,1},{1,0},{2,3},{3,2},{4,5},{5,4},{6,7},{7,6},{8,9},{9,8},{10,11... | collective-permute-start | bytes 98312 | tf_op jit(solution)/shard_map/ppermute | solution.py:222

commit v8 on v7

--- a/solution.py
+++ b/solution.py
@@ -181,28 +181,33 @@
 
 
 def chip_kernel(*refs):
-    *block_refs, mine_ref, theirs_ref, ridge_ref, out_ref, held = refs
+    *block_refs, mine_ref, theirs_ref, ridge_ref, out_ref = refs
     position = lax.axis_index("blk")
     core = lax.axis_index("rep")
-    slots, tile_items, dim = held.shape
-    owned, cycle_size = out_ref.shape[0], slots // 2
+    tile_items = block_refs[0].shape[0]
+    owned = out_ref.shape[0]
+    cycle_size = (mine_ref.shape[0] - tile_items) // (2 * owned)
+    blocks = [mine_ref[:tile_items], theirs_ref[:tile_items]]
+    slots = [position, cycle_size + position]
     for number, rules in enumerate(EXCHANGES):
         *rules, across = rules
         places = [source_slot(rule, position) for rule in rules]
         places = places[::-1] if across else places
-        direct, passed = block_refs[number], block_refs[len(EXCHANGES) + number]
-        held[jnp.where(core == 0, places[0], places[1])] = direct[...]
-        held[jnp.where(core == 0, places[1], places[0])] = passed[...]
-    held[position] = mine_ref[:tile_items]
-    held[cycle_size + position] = theirs_ref[:tile_items]
-    factors = held[...].reshape(-1, dim)
+        blocks += [block_refs[number][...], block_refs[len(EXCHANGES) + number][...]]
+        slots += [
+            jnp.where(core == 0, places[0], places[1]),
+            jnp.where(core == 0, places[1], places[0]),
+        ]
+    factors = jnp.concatenate(blocks, axis=0)
 
     def joined_tiles(kind):
-        rows = [
-            pl.ds(tile_items + (kind * cycle_size + source) * owned, owned)
-            for source in range(cycle_size)
-        ]
-        return jnp.concatenate([ref[row] for ref in (mine_ref, theirs_ref) for row in rows], axis=1)
+        tiles = []
+        for slot in slots:
+            source = lax.rem(slot, cycle_size)
+            start = tile_items + (kind * cycle_size + source) * owned
+            rows = pl.ds(pl.multiple_of(start, owned), owned)
+            tiles.append(jnp.where(slot < cycle_size, mine_ref[rows], theirs_ref[rows]))
+        return jnp.concatenate(tiles, axis=1)
 
     weighted = joined_tiles(0).astype(jnp.float32)
     total = conjugate_gradient(factors, weighted, joined_tiles(1), ridge_ref[...])
@@ -253,7 +258,6 @@
         out_shape=jax.ShapeDtypeStruct((owned, dim // 2), jnp.float32),
         in_specs=[VMEM] * (3 + len(direct) + len(passed)),
         out_specs=VMEM,
-        scratch_shapes=[pltpu.VMEM((2 * cycle_size, tile_items, dim), jnp.bfloat16)],
         compiler_params=pltpu.CompilerParams(vmem_limit_bytes=8 * 1024 * 1024),
     )(*direct, *passed, mine, theirs, ridge)
 

time: 13.6 us -> 13.6 us (level)
  no operation moved by 1% of the time
where the time goes in v8:
time: 13.6 us; the launch traced here: 13.4 us
  starting transfers between devices  9.49 us (70%)
  Pallas kernels  3.04 us (22%)
  waiting for transfers between devices  0.87 us (6%)
    ppermute x3, starting transfers between devices, chip_shards(): lax.ppermute(item_factors, PLACE, exchange_route(rules))  6.43 us
    pallas_call x1, Pallas kernels, chip_shards(): pl.pallas_call(chip_kernel, out_shape=jax.ShapeDtypeStruct((owned, dim //...  2.05 us
    ppermute x1, starting transfers between devices, chip_shards(): lax.ppermute(theirs, PLACE, exchange_route((*((ADD, 0, 1),) * 2, PACKET_A...  1.64 us
    ppermute x3, starting transfers between devices, chip_shards(): passed = [lax.ppermute(block, 'rep', swap) for block in direct]  1.42 us
    pallas_call x1, Pallas kernels, chip_shards(): pl.pallas_call(packet_kernel, out_shape=(packet, packet, ridge), in_specs...  0.99 us
    ppermute x3, waiting for transfers between devices, chip_shards(): passed = [lax.ppermute(block, 'rep', swap) for block in direct]  0.86 us
  transfers between devices with their start and end apart: 7, of which 2 were waited for; matrix products, arithmetic and copies ran while one was open for 0% of the time, Pallas kernels for 7%

profile of v8, /device:TPU:0, one launch (start us, length us, event | category | flops | bytes accessed | tf_op | source)
XLA Modules:
  0.0 13.4 jit_solution(13703867175486213304)
XLA Ops:
  0.0 4.4 %collective-permute-start = (bf16[128,128]{1,0:T(8,128)(2,1)}, bf16[128,128]{1,0:T(8,128)(2,1)S(1)}, u32[]{:S(2)}, u32[]{:S(2)}) collective-permute-start(bf16[128,128]{1,0:T(8,128)(2,1)} %factors_ref.1), channel_id=1, source_target_pairs={{0,11},{2,9},{4,15},{6,13},{8,3},{10,1},{12,7},{14,5},{1,4},{3,6},... | collective-permute-start | bytes 98312 | tf_op jit(solution)/shard_map/ppermute | solution.py:226
  4.4 1.5 %collective-permute-start.1 = (bf16[128,128]{1,0:T(8,128)(2,1)}, bf16[128,128]{1,0:T(8,128)(2,1)S(1)}, u32[]{:S(2)}, u32[]{:S(2)}) collective-permute-start(bf16[128,128]{1,0:T(8,128)(2,1)} %factors_ref.1), channel_id=1, source_target_pairs={{0,6},{2,4},{4,2},{6,0},{8,14},{10,12},{12,10},{14,8},{1,15},{3,13... | collective-permute-start | bytes 98312 | tf_op jit(solution)/shard_map/ppermute | solution.py:226
  6.0 0.5 %collective-permute-start.2 = (bf16[128,128]{1,0:T(8,128)(2,1)}, bf16[128,128]{1,0:T(8,128)(2,1)S(1)}, u32[]{:S(2)}, u32[]{:S(2)}) collective-permute-start(bf16[128,128]{1,0:T(8,128)(2,1)} %factors_ref.1), channel_id=1, source_target_pairs={{0,9},{2,11},{4,13},{6,15},{8,1},{10,3},{12,5},{14,7},{1,12},{3,14... | collective-permute-start | bytes 98312 | tf_op jit(solution)/shard_map/ppermute | solution.py:226
  6.4 0.0 collective-permute-done.earlier_ref.refs_0_
  6.4 1.0 %shard_map.55 = (bf16[256,128]{1,0:T(8,128)(2,1)S(1)}, bf16[256,128]{1,0:T(8,128)(2,1)S(1)}, f32[16,128]{1,0:T(8,128)S(1)}) custom-call(s32[4]{0:T(128)} %bitcast.6, bf16[128,128]{1,0:T(8,128)(2,1)} %bitcast.4, bf16[128,128]{1,0:T(8,128)(2,1)} %bitcast.5, bf16[128,128]{1,0:T(8,128)(2,1)} %factors_ref.1, s32[1,32]{1,0:T(1,128)} %bitcast.7, ...), custom_call_target="tpu_custom_call" | custom-call | tf_op jit(solution)/shard_map/pallas_call | solution.py:238
  7.4 1.6 %collective-permute-start.6 = (bf16[256,128]{1,0:T(8,128)(2,1)S(1)}, bf16[256,128]{1,0:T(8,128)(2,1)S(1)}, u32[]{:S(2)}, u32[]{:S(2)}) collective-permute-start(bf16[256,128]{1,0:T(8,128)(2,1)S(1)} %get-tuple-element.9), channel_id=1, source_target_pairs={{0,3},{2,1},{4,7},{6,5},{8,11},{10,9},{12,15},{14,13},{1,2},{3,0},... | collective-permute-start | bytes 196616 | tf_op jit(solution)/shard_map/ppermute | solution.py:255
  9.1 0.4 %collective-permute-start.3 = (bf16[128,128]{1,0:T(8,128)(2,1)S(1)}, bf16[128,128]{1,0:T(8,128)(2,1)S(1)}, u32[]{:S(2)}, u32[]{:S(2)}) collective-permute-start(bf16[128,128]{1,0:T(8,128)(2,1)S(1)} %collective-permute-done.earlier_ref.refs_0_), channel_id=1, source_target_pairs={{0,1},{1,0},{2,3},{3,2},{4,5},{5,4},{6,7},{7,6},{8,9},{9,8},{10,11... | collective-permute-start | bytes 98312 | tf_op jit(solution)/shard_map/ppermute | solution.py:227
  9.5 0.0 collective-permute-done.1.refs_1_
  9.5 0.1 collective-permute-start.4
  9.6 0.0 collective-permute-done.2.refs_2_
  9.6 0.9 %collective-permute-start.5 = (bf16[128,128]{1,0:T(8,128)(2,1)S(1)}, bf16[128,128]{1,0:T(8,128)(2,1)S(1)}, u32[]{:S(2)}, u32[]{:S(2)}) collective-permute-start(bf16[128,128]{1,0:T(8,128)(2,1)S(1)} %collective-permute-done.2.refs_2_), channel_id=1, source_target_pairs={{0,1},{1,0},{2,3},{3,2},{4,5},{5,4},{6,7},{7,6},{8,9},{9,8},{10,11... | collective-permute-start | bytes 98312 | tf_op jit(solution)/shard_map/ppermute | solution.py:227
  10.5 0.0 collective-permute-done.3.refs_3_
  10.5 0.2 %collective-permute-done.4.refs_4_ = bf16[128,128]{1,0:T(8,128)(2,1)S(1)} collective-permute-done((bf16[128,128]{1,0:T(8,128)(2,1)S(1)}, bf16[128,128]{1,0:T(8,128)(2,1)S(1)}, u32[]{:S(2)}, u32[]{:S(2)}) %collective-permute-start.4) | collective-permute-done | bytes 32800 | tf_op jit(solution)/shard_map/ppermute | solution.py:227
  10.7 0.7 %collective-permute-done.5.refs_5_ = bf16[128,128]{1,0:T(8,128)(2,1)S(1)} collective-permute-done((bf16[128,128]{1,0:T(8,128)(2,1)S(1)}, bf16[128,128]{1,0:T(8,128)(2,1)S(1)}, u32[]{:S(2)}, u32[]{:S(2)}) %collective-permute-start.5) | collective-permute-done | bytes 32800 | tf_op jit(solution)/shard_map/ppermute | solution.py:227
  11.4 0.0 collective-permute-done.6.refs_7_
  11.4 2.1 %shard_map.56 = f32[16,64]{1,0:T(8,128)} custom-call(bf16[128,128]{1,0:T(8,128)(2,1)S(1)} %collective-permute-done.earlier_ref.refs_0_, bf16[128,128]{1,0:T(8,128)(2,1)S(1)} %collective-permute-done.1.refs_1_, bf16[128,128]{1,0:T(8,128)(2,1)S(1)} %collective-permute-done.2.refs_2_, bf16[128,128]{1,0:T(8,128)(2,1)S(1)} %collective-permute-done.3.refs_3_, ...), custom_call_target="tpu_custom_call" | custom-call | tf_op jit(solution)/shard_map/pallas_call | solution.py:256
Async XLA Ops:
  0.0 6.4 %collective-permute-start = (bf16[128,128]{1,0:T(8,128)(2,1)}, bf16[128,128]{1,0:T(8,128)(2,1)S(1)}, u32[]{:S(2)}, u32[]{:S(2)}) collective-permute-start(bf16[128,128]{1,0:T(8,128)(2,1)} %factors_ref.1), channel_id=1, source_target_pairs={{0,11},{2,9},{4,15},{6,13},{8,3},{10,1},{12,7},{14,5},{1,4},{3,6},... | collective-permute-start | bytes 98312 | tf_op jit(solution)/shard_map/ppermute | solution.py:226
  4.4 5.1 %collective-permute-start.1 = (bf16[128,128]{1,0:T(8,128)(2,1)}, bf16[128,128]{1,0:T(8,128)(2,1)S(1)}, u32[]{:S(2)}, u32[]{:S(2)}) collective-permute-start(bf16[128,128]{1,0:T(8,128)(2,1)} %factors_ref.1), channel_id=1, source_target_pairs={{0,6},{2,4},{4,2},{6,0},{8,14},{10,12},{12,10},{14,8},{1,15},{3,13... | collective-permute-start | bytes 98312 | tf_op jit(solution)/shard_map/ppermute | solution.py:226
  6.0 3.6 %collective-permute-start.2 = (bf16[128,128]{1,0:T(8,128)(2,1)}, bf16[128,128]{1,0:T(8,128)(2,1)S(1)}, u32[]{:S(2)}, u32[]{:S(2)}) collective-permute-start(bf16[128,128]{1,0:T(8,128)(2,1)} %factors_ref.1), channel_id=1, source_target_pairs={{0,9},{2,11},{4,13},{6,15},{8,1},{10,3},{12,5},{14,7},{1,12},{3,14... | collective-permute-start | bytes 98312 | tf_op jit(solution)/shard_map/ppermute | solution.py:226
  7.4 3.9 %collective-permute-start.6 = (bf16[256,128]{1,0:T(8,128)(2,1)S(1)}, bf16[256,128]{1,0:T(8,128)(2,1)S(1)}, u32[]{:S(2)}, u32[]{:S(2)}) collective-permute-start(bf16[256,128]{1,0:T(8,128)(2,1)S(1)} %get-tuple-element.9), channel_id=1, source_target_pairs={{0,3},{2,1},{4,7},{6,5},{8,11},{10,9},{12,15},{14,13},{1,2},{3,0},... | collective-permute-start | bytes 196616 | tf_op jit(solution)/shard_map/ppermute | solution.py:255
  9.1 1.4 %collective-permute-start.3 = (bf16[128,128]{1,0:T(8,128)(2,1)S(1)}, bf16[128,128]{1,0:T(8,128)(2,1)S(1)}, u32[]{:S(2)}, u32[]{:S(2)}) collective-permute-start(bf16[128,128]{1,0:T(8,128)(2,1)S(1)} %collective-permute-done.earlier_ref.refs_0_), channel_id=1, source_target_pairs={{0,1},{1,0},{2,3},{3,2},{4,5},{5,4},{6,7},{7,6},{8,9},{9,8},{10,11... | collective-permute-start | bytes 98312 | tf_op jit(solution)/shard_map/ppermute | solution.py:227
  9.5 1.2 %collective-permute-start.4 = (bf16[128,128]{1,0:T(8,128)(2,1)S(1)}, bf16[128,128]{1,0:T(8,128)(2,1)S(1)}, u32[]{:S(2)}, u32[]{:S(2)}) collective-permute-start(bf16[128,128]{1,0:T(8,128)(2,1)S(1)} %collective-permute-done.1.refs_1_), channel_id=1, source_target_pairs={{0,1},{1,0},{2,3},{3,2},{4,5},{5,4},{6,7},{7,6},{8,9},{9,8},{10,11... | collective-permute-start | bytes 98312 | tf_op jit(solution)/shard_map/ppermute | solution.py:227
  9.6 1.8 %collective-permute-start.5 = (bf16[128,128]{1,0:T(8,128)(2,1)S(1)}, bf16[128,128]{1,0:T(8,128)(2,1)S(1)}, u32[]{:S(2)}, u32[]{:S(2)}) collective-permute-start(bf16[128,128]{1,0:T(8,128)(2,1)S(1)} %collective-permute-done.2.refs_2_), channel_id=1, source_target_pairs={{0,1},{1,0},{2,3},{3,2},{4,5},{5,4},{6,7},{7,6},{8,9},{9,8},{10,11... | collective-permute-start | bytes 98312 | tf_op jit(solution)/shard_map/ppermute | solution.py:227
